TPU v7x, 32 devices: a whole 2x2x4 slice. The times are simulated.
32 devices in a mesh: ctx: 4 (over z), ep: 8 (over y, x, core).
Axes of the slice: x: 2, y: 2, z: 4, core: 2. Of those that a mesh axis runs over, the one named last changes fastest.
Arguments:
- queries: bfloat16 [1024, 8192], P('ctx', 'ep'), may hold values from -6 to 6
- key_rows: bfloat16 [1024, 8192], P('ctx', 'ep'), may hold values from -6 to 6
- value_rows: bfloat16 [1024, 8192], P('ctx', 'ep'), may hold values from -6 to 6
- log_decay: float32 [1024, 64], P('ctx', 'ep'), may hold values from -1 to 0
- out_weight: bfloat16 [6144, 8192], P('ep'), may hold values from -0.0625 to 0.0625
- expert_ids: int32 [1024, 2], P('ctx'), may hold values from 0 to 7, all different within a row; in each aligned block of 256 rows (0 to 255, 256 to 511, ...) at most 128 rows name the same one
- flagged: int32 [256], P('ctx'), may hold values from 0 to 1023, as said below
- direction: float32 [6144], P('ep'), as said below
Outputs:
- expert_tiles: bfloat16 [8, 512, 6144], P('ep', 'ctx')
Inputs may be any that keep to these rules, and one draw needn't show every extreme that they name: `expert_ids`: each row names 2 different experts; among the 256 rows of one block of the sequence no expert is named more than 128 times, a bound that some block reaches. `flagged`: entries 64 * b to 64 * b + 63 are distinct rows of block b of 256 rows. `direction`: not all zero.
All inputs are finite; a program needn't handle non-finite values.
Results may differ from a plain program's by a relative error of at most 0.0059.
Values may be sent and summed in bfloat16 or wider, within the bound.
A program may use at most 64 MiB of HBM per device.

v0:
```python
import jax
import jax.numpy as jnp
from jax import lax
from jax.sharding import PartitionSpec as P

HEAD = 128
TOP = 2
EXP_DEV = 1
SUB = 256


def passed_along(value, axis, steps):
    count = lax.axis_size(axis)
    leading, last = (max(0, -steps), min(count, count - steps))
    return lax.ppermute(value, axis, [(source, source + steps) for source in range(leading, last)])


def local_step(carried_in, pieces):
    kv_state, offset = carried_in
    query_sub, key_sub, value_sub, decay_sub = pieces
    sub_rows = query_sub.shape[0]
    cumulated = jnp.cumsum(decay_sub, axis=0)
    scores = jnp.einsum("thd,shd->hts", query_sub, key_sub, preferred_element_type=jnp.float32)
    spread = jnp.transpose(cumulated)
    decay_gaps = jnp.minimum(spread[:, :, None] - spread[:, None, :], 0.0)
    causal = (
        jnp.arange(sub_rows, dtype=jnp.int32)[:, None]
        >= jnp.arange(sub_rows, dtype=jnp.int32)[None, :]
    )
    weights = jnp.where(causal[None], scores * jnp.exp(decay_gaps), 0.0).astype(jnp.bfloat16)
    inside = jnp.einsum("hts,shd->thd", weights, value_sub, preferred_element_type=jnp.float32)
    scaled = query_sub.astype(jnp.float32) * jnp.exp(cumulated)[:, :, None]
    carried = jnp.einsum("thd,hde->the", scaled, kv_state, precision=lax.Precision.HIGHEST)
    last_decay = cumulated[-1]
    key_scaled = (
        key_sub.astype(jnp.float32) * jnp.exp(last_decay[None, :] - cumulated)[:, :, None]
    ).astype(jnp.bfloat16)
    update = jnp.einsum("shd,she->hde", key_scaled, value_sub, preferred_element_type=jnp.float32)
    kv_state = jnp.exp(last_decay)[:, None, None] * kv_state + update
    reach_decay = jnp.exp(offset[None, :] + cumulated)
    return ((kv_state, offset + last_decay), (inside + carried, reach_decay))


def normalize(outputs):
    mean_square = jnp.mean(outputs * outputs, axis=-1, keepdims=True)
    return (outputs * lax.rsqrt(mean_square + 1e-06)).astype(jnp.bfloat16)


def local(queries, key_rows, value_rows, log_decay, out_weight, expert_ids, flagged, direction):
    block_rows = queries.shape[0]
    local_width = queries.shape[1]
    local_heads = local_width // HEAD
    sub_count = block_rows // SUB
    model_cols = out_weight.shape[0]

    def shaped(operand):
        return operand.reshape(sub_count, SUB, local_heads, HEAD)

    start_state = (
        jnp.zeros((local_heads, HEAD, HEAD), jnp.float32),
        jnp.zeros((local_heads,), jnp.float32),
    )
    scanned = lax.scan(
        local_step,
        start_state,
        (
            shaped(queries),
            shaped(key_rows),
            shaped(value_rows),
            log_decay.reshape(sub_count, SUB, local_heads),
        ),
    )
    local_state, total_decay = scanned[0]
    partial_out, reach_decay = scanned[1]
    block_gain = jnp.exp(total_decay)

    def pass_state(hop_index, incoming):
        passed = block_gain[:, None, None] * incoming + local_state
        return passed_along(passed, "ctx", 1)

    incoming = lax.fori_loop(0, lax.axis_size("ctx") - 1, pass_state, jnp.zeros_like(local_state))
    scaled = shaped(queries).astype(jnp.float32) * reach_decay[..., None]
    outputs = partial_out + jnp.einsum(
        "cthd,hde->cthe", scaled, incoming, precision=lax.Precision.HIGHEST
    )
    attended = normalize(outputs).reshape(block_rows, local_width)
    projected = lax.dot_general(
        lax.all_gather(attended, "ep", axis=1, tiled=True),
        out_weight,
        (((1,), (1,)), ((), ())),
        preferred_element_type=jnp.float32,
    ).astype(jnp.bfloat16)
    ctx_start = lax.axis_index("ctx") * block_rows
    local_flags = flagged - ctx_start
    experts_all = lax.axis_size("ep") * EXP_DEV
    capacity = 2 * block_rows * TOP // experts_all
    flat_ids = expert_ids.reshape(-1)
    matches = (flat_ids[:, None] == jnp.arange(experts_all, dtype=jnp.int32)[None, :]).astype(
        jnp.int32
    )
    slot_index = jnp.sum((jnp.cumsum(matches, axis=0) - matches) * matches, axis=1)
    source = jnp.arange(block_rows * TOP, dtype=jnp.int32) // TOP
    picked = projected[local_flags].astype(jnp.float32)
    partial_dot = jnp.dot(picked, direction, precision=lax.Precision.HIGHEST)
    products, norm_square = lax.psum((partial_dot, jnp.sum(direction * direction)), "ep")
    norm_square = norm_square + 1e-06
    removed = (picked - (products / norm_square)[:, None] * direction[None, :]).astype(jnp.bfloat16)
    ablated = projected.at[local_flags].set(removed)
    tile_rows = (
        jnp.zeros((experts_all, capacity, model_cols), jnp.bfloat16)
        .at[flat_ids, slot_index]
        .set(ablated[source])
    )
    return lax.all_to_all(tile_rows, "ep", split_axis=0, concat_axis=2, tiled=True)


def solution(mesh):
    placed = (
        P("ctx", "ep"),
        P("ctx", "ep"),
        P("ctx", "ep"),
        P("ctx", "ep"),
        P("ep", None),
        P("ctx", None),
        P("ctx"),
        P("ep"),
    )
    return jax.shard_map(
        local, mesh=mesh, in_specs=placed, out_specs=P("ep", "ctx", None), check_vma=False
    )
```

profile of v0, /device:TPU:25, one launch (start us, length us, event | category | flops | bytes accessed | tf_op | source)
XLA Modules:
  0.0 192.4 jit_solution(6032792826790357492)
XLA Ops:
  6.5 1.3 reduce-window.16
  7.8 0.2 slice_reduce_fusion.1
  8.1 0.2 slice_reduce_fusion.2
  8.5 1.2 copy.39
  9.8 1.2 convolution_bitcast_fusion.1
  11.0 1.3 convolution_add_fusion
  12.4 41.7 %while.2 = (s32[]{:T(128)}, f32[8,128,128]{2,1,0:T(8,128)S(1)}, f32[8]{0:T(128)S(1)}, f32[8,128,128]{2,1,0:T(8,128)S(1)}, s32[]{:T(128)}) while((s32[]{:T(128)}, f32[8,128,128]{2,1,0:T(8,128)S(1)}, f32[8]{0:T(128)S(1)}, f32[8,128,128]{2,1,0:T(8,128)S(1)}, s32[]{:T(128)}) %tuple.23), condition=%wide.region_6.7_spmd, body=%wide.region_5.6_spmd.sunk | while | flops 262146 | bytes 3670149 | solution.py:81
  12.6 1.3 collective-permute-start
  13.9 13.4 %collective-permute-done = f32[8,128,128]{2,1,0:T(8,128)S(1)} collective-permute-done((f32[8,128,128]{2,1,0:T(8,128)S(1)}, f32[8,128,128]{2,1,0:T(8,128)S(1)}, u32[]{:S(2)}, u32[]{:S(2)}) %collective-permute-start) | collective-permute-done | bytes 524320 | tf_op jit(solution)/shard_map/while/body/eval_jaxpr/ppermute | solution.py:15
  27.4 1.3 collective-permute-start
  28.7 12.5 %collective-permute-done = f32[8,128,128]{2,1,0:T(8,128)S(1)} collective-permute-done((f32[8,128,128]{2,1,0:T(8,128)S(1)}, f32[8,128,128]{2,1,0:T(8,128)S(1)}, u32[]{:S(2)}, u32[]{:S(2)}) %collective-permute-start) | collective-permute-done | bytes 524320 | tf_op jit(solution)/shard_map/while/body/eval_jaxpr/ppermute | solution.py:15
  41.3 1.3 collective-permute-start
  42.6 11.5 %collective-permute-done = f32[8,128,128]{2,1,0:T(8,128)S(1)} collective-permute-done((f32[8,128,128]{2,1,0:T(8,128)S(1)}, f32[8,128,128]{2,1,0:T(8,128)S(1)}, u32[]{:S(2)}, u32[]{:S(2)}) %collective-permute-start) | collective-permute-done | bytes 524320 | tf_op jit(solution)/shard_map/while/body/eval_jaxpr/ppermute | solution.py:15
  54.1 2.4 %convolution_bitcast_fusion = f32[1,256,8,128]{1,3,2,0:T(8,128)} fusion(f32[8,128,128]{2,1,0:T(8,128)S(1)} %get-tuple-element.52, f32[256,8]{0,1:T(8,128)S(1)} %get-tuple-element.65, bf16[256,1024]{1,0:T(8,128)(2,1)S(1)} %copy-done), kind=kOutput, calls=%fused_computation.10 | convolution fusion | flops 403177472 | bytes 2105344 | tf_op jit(solution)/shard_map/cthd,hde->cthe/dot_general | solution.py:83
  56.5 2.4 %multiply_reduce_fusion = (f32[256,8]{0,1:T(8,128)S(1)}, f32[1,256,8,128]{1,3,2,0:T(8,128)S(1)}) fusion(f32[1,256,8,128]{1,3,2,0:T(8,128)} %convolution_bitcast_fusion, f32[256,8,128]{0,2,1:T(8,128)S(1)} %convolution_bitcast_fusion.1, bf16[256,8,128]{0,2,1:T(8,128)(2,1)S(1)} %bitcast.96, f32[8,256]{1,0:T(8,128)S(1)} %add_bitcast_fusion.1, ...), kind=kOutput, calls=%fused_computation.17 | convolution fusion | flops 272103424 | bytes 4800512 | tf_op jit(solution)/shard_map/while/body/eval_jaxpr/hts,shd->thd/dot_general | solution.py:31
  58.9 0.9 multiply_convert_fusion
  60.0 0.1 eq.29
  60.1 0.1 eq.25
  60.3 0.1 reshape.194
  60.5 1.1 reduce-window.14
  61.6 0.2 slice_reduce_fusion
  61.9 0.6 multiply_reduce_fusion.1
  62.7 38.2 %all-gather.2.cloned.1.call-done = bf16[256,8192]{0,1:T(8,128)(2,1)} async-done(((bf16[256,1024]{0,1:T(8,128)(2,1)}), bf16[256,8192]{0,1:T(8,128)(2,1)}) %all-gather.2.cloned.1.call-update) | async-done | bytes 4194320 | tf_op jit(solution)/shard_map/all_gather | solution.py:88
  100.8 9.3 %convolution_convert_fusion = bf16[256,768]{1,0:T(8,128)(2,1)S(1)} fusion(bf16[256,8192]{0,1:T(8,128)(2,1)} %all-gather.2.cloned.1.call-done, bf16[768,8192]{1,0:T(8,128)(2,1)} %param.14), kind=kOutput, calls=%fused_computation.13 | convolution fusion | flops 3221422080 | bytes 17170432 | tf_op jit(solution)/shard_map/dot_general | solution.py:87
  110.2 0.7 gather_fusion
  111.0 12.1 %all-reduce = (f32[64]{0:T(128)S(1)}, f32[]{:T(128)}) all-reduce(f32[64]{0:T(128)S(1)} %convolution_bitcast_fusion.2, f32[]{:T(128)} %multiply_reduce_fusion.1), channel_id=1, replica_groups=mesh['ctx'=4,'ep'=8] {'ep'}, use_global_device_ids=true, to_apply=%region_8.9 | all-reduce | flops 65 | bytes 520 | tf_op jit(solution)/shard_map/psum | solution.py:105
  123.8 1.2 scatter_custom_fusion
  124.9 2.0 %gather_fusion.1 = bf16[512,768]{1,0:T(8,128)(2,1)S(1)} fusion(bf16[256,768]{1,0:T(8,128)(2,1)S(1)} %scatter_custom_fusion, s32[1024]{0:T(1024)S(1)} %pad_clamp_fusion), kind=kCustom, calls=%fused_computation.1 | custom fusion | bytes 1574912 | tf_op jit(solution)/shard_map/gather | solution.py:112
  127.1 30.2 %scatter_fusion = bf16[8,128,768]{2,1,0:T(8,128)(2,1)S(1)} fusion(bf16[8,128,768]{2,1,0:T(8,128)(2,1)S(1)} %broadcast_in_dim.44, s32[512]{0:T(512)S(1)} %bitcast.91, bf16[512,768]{1,0:T(8,128)(2,1)S(1)} %gather_fusion.1), kind=kCustom, calls=%fused_computation.3 | custom fusion | bytes 2363392 | tf_op jit(solution)/shard_map/scatter | solution.py:112
  157.3 24.7 %all_to_all.18 = bf16[8,128,768]{2,1,0:T(8,128)(2,1)} all-to-all(bf16[8,128,768]{2,1,0:T(8,128)(2,1)S(1)} %scatter_fusion), channel_id=1, replica_groups=mesh['ctx'=4,'ep'=8] {'ep'}, dimensions={0} | all-to-all | bytes 3145728 | tf_op jit(solution)/shard_map/all_to_all | solution.py:114
  182.1 1.9 copy.35
  184.0 1.6 copy.36
  (40 shorter events, 1.3 us)
Async XLA Ops:
  6.5 3.2 %copy-start = (bf16[256,1024]{1,0:T(8,128)(2,1)S(1)}, bf16[256,1024]{1,0:T(8,128)(2,1)}, u32[]{:S(2)}) copy-start(bf16[256,1024]{1,0:T(8,128)(2,1)} %param.10) | copy-start | bytes 1572868
  6.5 94.3 %all-gather.2.cloned.1.call-start = ((), (), s32[]{:S(2)}) async-start(), calls=%async_computation.1 | async-start | bytes 4718592 | tf_op jit(solution)/shard_map/all_gather | solution.py:88
  9.8 2.6 %copy-start.1 = (bf16[256,1024]{0,1:T(8,128)(2,1)}, bf16[256,1024]{0,1:T(8,128)(2,1)S(1)}, u32[]{:S(2)}) copy-start(bf16[256,1024]{0,1:T(8,128)(2,1)S(1)} %copy.39) | copy-start | bytes 1572868
  12.6 14.7 %collective-permute-start = (f32[8,128,128]{2,1,0:T(8,128)S(1)}, f32[8,128,128]{2,1,0:T(8,128)S(1)}, u32[]{:S(2)}, u32[]{:S(2)}) collective-permute-start(f32[8,128,128]{2,1,0:T(8,128)S(1)} %multiply_add_fusion.2), channel_id=1, source_target_pairs={{0,8},{8,16},{16,24},{1,9},{9,17},{17,25},{2,10},{10,18},{18,26},{... | collective-permute-start | bytes 1572872 | tf_op jit(solution)/shard_map/while/body/eval_jaxpr/ppermute | solution.py:15
  27.4 13.8 %collective-permute-start = (f32[8,128,128]{2,1,0:T(8,128)S(1)}, f32[8,128,128]{2,1,0:T(8,128)S(1)}, u32[]{:S(2)}, u32[]{:S(2)}) collective-permute-start(f32[8,128,128]{2,1,0:T(8,128)S(1)} %multiply_add_fusion.2), channel_id=1, source_target_pairs={{0,8},{8,16},{16,24},{1,9},{9,17},{17,25},{2,10},{10,18},{18,26},{... | collective-permute-start | bytes 1572872 | tf_op jit(solution)/shard_map/while/body/eval_jaxpr/ppermute | solution.py:15
  41.3 12.8 %collective-permute-start = (f32[8,128,128]{2,1,0:T(8,128)S(1)}, f32[8,128,128]{2,1,0:T(8,128)S(1)}, u32[]{:S(2)}, u32[]{:S(2)}) collective-permute-start(f32[8,128,128]{2,1,0:T(8,128)S(1)} %multiply_add_fusion.2), channel_id=1, source_target_pairs={{0,8},{8,16},{16,24},{1,9},{9,17},{17,25},{2,10},{10,18},{18,26},{... | collective-permute-start | bytes 1572872 | tf_op jit(solution)/shard_map/while/body/eval_jaxpr/ppermute | solution.py:15
  54.1 2.4 %copy-start.2 = (bf16[256,1024]{0,1:T(8,128)(2,1)S(1)}, bf16[256,1024]{0,1:T(8,128)(2,1)}, u32[]{:S(2)}) copy-start(bf16[256,1024]{0,1:T(8,128)(2,1)} %copy-done.1) | copy-start | bytes 1572868
  58.9 1.0 copy-start.4
  58.9 1.6 copy-start.3
  58.9 3.0 %copy-start.5 = (s32[64]{0:T(128)S(1)}, s32[64]{0:T(128)}, u32[]{:S(2)}) copy-start(s32[64]{0:T(128)} %param.16) | copy-start | bytes 772
Sparse Core Ops, SparseCore 0:
  60.0 40.8 all-gather.1
where the time goes:
time: 195 us; the launch traced here: 192 us
  waiting for transfers between devices  75.6 us (39%)
  local copies, waits for them, and re-layouts  39 us (20%)
  blocking collectives  36.8 us (19%)
  matrix products  16.8 us (9%)
  between operations  14.3 us (7%)
  other arithmetic  5.98 us (3%)
  starting transfers between devices  3.88 us (2%)
    all_gather x1, waiting for transfers between devices, local(): lax.all_gather(attended, 'ep', axis=1, tiled=True)  38.2 us
    ppermute x3, waiting for transfers between devices, passed_along(): lax.ppermute(value, axis, [(source, source + steps) for source in range(l...  37.4 us
    scatter x1, local copies, waits for them, and re-layouts, local(): tile_rows = jnp.zeros((experts_all, capacity, model_cols), jnp.bfloat16)....  30.2 us
    all_to_all x1, blocking collectives, local(): lax.all_to_all(tile_rows, 'ep', split_axis=0, concat_axis=2, tiled=True)  24.7 us
    psum x1, blocking collectives, local(): lax.psum((partial_dot, jnp.sum(direction * direction)), 'ep')  12.1 us
    dot_general x1, matrix products, local(): lax.dot_general(lax.all_gather(attended, 'ep', axis=1, tiled=True), out_w...  9.32 us
  transfers between devices with their start and end apart: 4, of which 4 were waited for; matrix products, arithmetic and copies ran while one was open for 1% of the time, Pallas kernels for 0%

commit v1 on v0

--- a/solution.py
+++ b/solution.py
@@ -76,7 +76,7 @@
 
     def pass_state(hop_index, incoming):
         passed = block_gain[:, None, None] * incoming + local_state
-        return passed_along(passed, "ctx", 1)
+        return passed_along(passed.astype(jnp.bfloat16), "ctx", 1).astype(jnp.float32)
 
     incoming = lax.fori_loop(0, lax.axis_size("ctx") - 1, pass_state, jnp.zeros_like(local_state))
     scaled = shaped(queries).astype(jnp.float32) * reach_decay[..., None]
@@ -94,24 +94,29 @@
     local_flags = flagged - ctx_start
     experts_all = lax.axis_size("ep") * EXP_DEV
     capacity = 2 * block_rows * TOP // experts_all
-    flat_ids = expert_ids.reshape(-1)
-    matches = (flat_ids[:, None] == jnp.arange(experts_all, dtype=jnp.int32)[None, :]).astype(
-        jnp.int32
-    )
-    slot_index = jnp.sum((jnp.cumsum(matches, axis=0) - matches) * matches, axis=1)
-    source = jnp.arange(block_rows * TOP, dtype=jnp.int32) // TOP
-    picked = projected[local_flags].astype(jnp.float32)
-    partial_dot = jnp.dot(picked, direction, precision=lax.Precision.HIGHEST)
-    products, norm_square = lax.psum((partial_dot, jnp.sum(direction * direction)), "ep")
-    norm_square = norm_square + 1e-06
-    removed = (picked - (products / norm_square)[:, None] * direction[None, :]).astype(jnp.bfloat16)
-    ablated = projected.at[local_flags].set(removed)
-    tile_rows = (
-        jnp.zeros((experts_all, capacity, model_cols), jnp.bfloat16)
-        .at[flat_ids, slot_index]
-        .set(ablated[source])
-    )
-    return lax.all_to_all(tile_rows, "ep", split_axis=0, concat_axis=2, tiled=True)
+    row_number = jnp.arange(block_rows, dtype=jnp.int32)
+    expert_number = jnp.arange(experts_all, dtype=jnp.int32)
+    named = jnp.any(expert_ids[:, :, None] == expert_number[None, None, :], axis=1)
+    before = (row_number[:, None] > row_number[None, :]).astype(jnp.bfloat16)
+    slot_index = jnp.dot(before, named.astype(jnp.bfloat16), preferred_element_type=jnp.float32)
+    slot_index = jnp.where(named, slot_index.astype(jnp.int32), -1).T
+    picks = slot_index[:, None, :] == jnp.arange(capacity, dtype=jnp.int32)[None, :, None]
+    tile_rows = jnp.einsum(
+        "ecr,rm->ecm",
+        picks.astype(jnp.bfloat16),
+        projected,
+        preferred_element_type=jnp.float32,
+    ).astype(jnp.bfloat16)
+    tiles = lax.all_to_all(tile_rows, "ep", split_axis=0, concat_axis=2, tiled=True)
+    row_flags = jnp.any(local_flags[:, None] == row_number[None, :], axis=0)
+    own_picks = lax.dynamic_slice_in_dim(picks, lax.axis_index("ep") * EXP_DEV, EXP_DEV, 0)
+    slot_flags = jnp.any(own_picks & row_flags[None, None, :], axis=2)
+    whole_direction = lax.all_gather(direction, "ep", tiled=True)
+    norm_square = jnp.sum(whole_direction * whole_direction) + 1e-06
+    rows = tiles.astype(jnp.float32)
+    products = jnp.sum(rows * whole_direction, axis=2)
+    removed = rows - (products / norm_square)[:, :, None] * whole_direction
+    return jnp.where(slot_flags[:, :, None], removed.astype(jnp.bfloat16), tiles)
 
 
 def solution(mesh):

time: 195 us -> 139 us (0.71)
  local copies, waits for them, and re-layouts: 39 us -> 4.75 us
  waiting for transfers between devices: 75.6 us -> 61.5 us
  blocking collectives: 36.8 us -> 24 us
  starting transfers between devices: 3.88 us -> 7.74 us
  matrix products: 16.8 us -> 18.8 us
    scatter x1 -> x0, local copies, waits for them, and re-layouts: 30.2 us -> none  [local(): tile_rows = jnp.zeros((experts_all, capacity, model_cols), jnp.bfloat16)....]
    all_to_all x1 -> x0, blocking collectives: 24.7 us -> none  [local(): lax.all_to_all(tile_rows, 'ep', split_axis=0, concat_axis=2, tiled=True)]
    all_gather x0 -> x1, blocking collectives: none -> 24 us  [local(): whole_direction = lax.all_gather(direction, 'ep', tiled=True)]
    ppermute x3, waiting for transfers between devices: 37.4 us -> 20.4 us  [passed_along(): lax.ppermute(value, axis, [(source, source + steps) for source in range(l...]
    psum x1 -> x0, blocking collectives: 12.1 us -> none  [local(): lax.psum((partial_dot, jnp.sum(direction * direction)), 'ep')]
    all_to_all x0 -> x1, starting transfers between devices: none -> 3.86 us  [local(): lax.all_to_all(tile_rows, 'ep', split_axis=0, concat_axis=2, tiled=True)]
    all_gather x1, waiting for transfers between devices: 38.2 us -> 41 us  [local(): lax.all_gather(attended, 'ep', axis=1, tiled=True)]
    gather x2 -> x0, local copies, waits for them, and re-layouts: 2.73 us -> none  [the longest x1 2.03 us: local(): ablated[source]]
  transfers between devices with their start and end apart: 4 -> 5, of which waited for: 4 -> 4; matrix products, arithmetic and copies ran while one was open for 1% -> 1% of each run, Pallas kernels for 0% -> 0%
where the time goes in v1:
time: 139 us; the launch traced here: 138 us
  waiting for transfers between devices  61.5 us (44%)
  blocking collectives  24 us (17%)
  matrix products  18.8 us (14%)
  between operations  14.2 us (10%)
  starting transfers between devices  7.74 us (6%)
  other arithmetic  6.58 us (5%)
  local copies, waits for them, and re-layouts  4.75 us (3%)
    all_gather x1, waiting for transfers between devices, local(): lax.all_gather(attended, 'ep', axis=1, tiled=True)  41 us
    all_gather x1, blocking collectives, local(): whole_direction = lax.all_gather(direction, 'ep', tiled=True)  24 us
    ppermute x3, waiting for transfers between devices, passed_along(): lax.ppermute(value, axis, [(source, source + steps) for source in range(l...  20.4 us
    dot_general x1, matrix products, local(): jnp.einsum('ecr,rm->ecm', picks.astype(jnp.bfloat16), projected, preferre...  11.2 us
    ppermute x3, starting transfers between devices, passed_along(): lax.ppermute(value, axis, [(source, source + steps) for source in range(l...  3.88 us
    all_to_all x1, starting transfers between devices, local(): lax.all_to_all(tile_rows, 'ep', split_axis=0, concat_axis=2, tiled=True)  3.86 us
  transfers between devices with their start and end apart: 5, of which 4 were waited for; matrix products, arithmetic and copies ran while one was open for 1% of the time, Pallas kernels for 0%

profile of v1, /device:TPU:25, one launch (start us, length us, event | category | flops | bytes accessed | tf_op | source)
XLA Modules:
  0.0 137.8 jit_solution(902418099010586200)
XLA Ops:
  6.5 1.3 reduce-window.6
  7.8 0.2 slice_reduce_fusion
  8.1 0.2 slice_reduce_fusion.1
  8.5 1.2 copy.54
  9.8 1.2 convolution_bitcast_fusion.1
  11.0 1.3 convolution_add_fusion
  12.4 24.9 %while.3 = (s32[]{:T(128)}, f32[8,128,128]{2,1,0:T(8,128)S(1)}, f32[8]{0:T(128)S(1)}, f32[8,128,128]{2,1,0:T(8,128)S(1)}, s32[]{:T(128)}, /*index=5*/s32[]{:T(128)}) while((s32[]{:T(128)}, f32[8,128,128]{2,1,0:T(8,128)S(1)}, f32[8]{0:T(128)S(1)}, f32[8,128,128]{2,1,0:T(8,128)S(1)}, s32[]{:T(128)}, /*index=5*/s32[]{:T(128)}) %tuple.27), condition=%wide.region_6.7_spmd.clone, body=%wide.region_5.6_spmd.clone.sunk | while | flops 655363 | bytes 3145879 | solution.py:81
  12.4 0.1 fusion.48
  12.5 1.3 collective-permute-start
  13.8 7.8 %collective-permute-done = bf16[8,128,128]{2,1,0:T(8,128)(2,1)S(1)} collective-permute-done((bf16[8,128,128]{2,1,0:T(8,128)(2,1)S(1)}, bf16[8,128,128]{2,1,0:T(8,128)(2,1)S(1)}, u32[]{:S(2)}, u32[]{:S(2)}) %collective-permute-start) | collective-permute-done | bytes 262176 | tf_op jit(solution)/shard_map/while/body/eval_jaxpr/ppermute | solution.py:15
  21.7 0.1 fusion.48
  21.8 1.3 collective-permute-start
  23.1 6.8 %collective-permute-done = bf16[8,128,128]{2,1,0:T(8,128)(2,1)S(1)} collective-permute-done((bf16[8,128,128]{2,1,0:T(8,128)(2,1)S(1)}, bf16[8,128,128]{2,1,0:T(8,128)(2,1)S(1)}, u32[]{:S(2)}, u32[]{:S(2)}) %collective-permute-start) | collective-permute-done | bytes 262176 | tf_op jit(solution)/shard_map/while/body/eval_jaxpr/ppermute | solution.py:15
  30.0 0.1 fusion.48
  30.1 1.3 collective-permute-start
  31.4 5.8 %collective-permute-done = bf16[8,128,128]{2,1,0:T(8,128)(2,1)S(1)} collective-permute-done((bf16[8,128,128]{2,1,0:T(8,128)(2,1)S(1)}, bf16[8,128,128]{2,1,0:T(8,128)(2,1)S(1)}, u32[]{:S(2)}, u32[]{:S(2)}) %collective-permute-start) | collective-permute-done | bytes 262176 | tf_op jit(solution)/shard_map/while/body/eval_jaxpr/ppermute | solution.py:15
  37.3 2.3 %convolution_bitcast_fusion = f32[1,256,8,128]{1,3,2,0:T(8,128)} fusion(f32[8,128,128]{2,1,0:T(8,128)S(1)} %get-tuple-element.52, f32[256,8]{0,1:T(8,128)S(1)} %get-tuple-element.78, bf16[256,1024]{1,0:T(8,128)(2,1)S(1)} %copy-done), kind=kOutput, calls=%fused_computation.12 | convolution fusion | flops 403177472 | bytes 2105344 | tf_op jit(solution)/shard_map/cthd,hde->cthe/dot_general | solution.py:83
  39.6 2.5 %multiply_reduce_fusion.1 = (f32[256,8]{0,1:T(8,128)S(1)}, f32[1,256,8,128]{1,3,2,0:T(8,128)S(1)}) fusion(f32[1,256,8,128]{1,3,2,0:T(8,128)} %convolution_bitcast_fusion, f32[256,8,128]{0,2,1:T(8,128)S(1)} %convolution_bitcast_fusion.1, bf16[256,8,128]{0,2,1:T(8,128)(2,1)} %bitcast.92, f32[8,256]{1,0:T(8,128)S(1)} %add_bitcast_fusion.1, ...), kind=kOutput, calls=%fused_computation.21 | convolution fusion | flops 272103424 | bytes 4800512 | tf_op jit(solution)/shard_map/while/body/eval_jaxpr/hts,shd->thd/dot_general | solution.py:31
  42.2 0.9 multiply_convert_fusion
  43.1 0.2 fusion.9
  43.3 41.0 %all-gather.3.cloned.1.call-done = bf16[256,8192]{0,1:T(8,128)(2,1)} async-done(((bf16[256,1024]{0,1:T(8,128)(2,1)}), bf16[256,8192]{0,1:T(8,128)(2,1)}) %all-gather.3.cloned.1.call-update) | async-done | bytes 4194320 | tf_op jit(solution)/shard_map/all_gather | solution.py:88
  84.3 11.2 %convolution_convert_fusion = bf16[8,128,768]{2,1,0:T(8,128)(2,1)} fusion(bf16[256,8192]{0,1:T(8,128)(2,1)} %all-gather.3.cloned.1.call-done, bf16[768,8192]{1,0:T(8,128)(2,1)} %param.14, s32[8,256]{1,0:T(8,128)S(1)} %fusion.9), kind=kOutput, calls=%fused_computation.7 | convolution fusion | flops 3625123840 | bytes 18358272 | tf_op jit(solution)/shard_map/ecr,rm->ecm/dot_general | solution.py:104
  95.5 3.9 %all-to-all-start = ((bf16[8,128,768]{2,1,0:T(8,128)(2,1)}), bf16[8,128,768]{2,1,0:T(8,128)(2,1)S(1)}, u32[]{:S(2)}, u32[]{:S(2)}) async-start(bf16[8,128,768]{2,1,0:T(8,128)(2,1)} %convolution_convert_fusion), calls=%async_computation | async-start | bytes 3145728 | tf_op jit(solution)/shard_map/all_to_all | solution.py:110
  99.4 24.0 %all-gather = f32[8,1,768]{2,1,0:T(1,128)S(1)} all-gather(f32[1,1,768]{2,1,0:T(1,128)S(1)} %reshape.220), channel_id=1, replica_groups=mesh['ctx'=4,'ep'=8] {'ep'}, dimensions={0}, use_global_device_ids=true | all-gather | bytes 27648 | tf_op jit(solution)/shard_map/all_gather | solution.py:114
  123.5 0.7 multiply_reduce_fusion.2
  124.9 0.1 fusion.30
  125.0 0.1 iota_compare_fusion
  125.1 0.1 and_reduce_fusion
  125.2 1.6 %copy.50 = bf16[1,128,8,768]{1,3,2,0:T(8,128)(2,1)} copy(bf16[1,128,8,768]{3,1,2,0:T(8,128)(2,1)S(1)} %bitcast.89) | data formatting | bytes 3145728 | tf_op jit(solution)/shard_map/all_to_all | solution.py:110
  126.8 0.4 multiply_reduce_fusion
  127.2 2.1 %fusion.2 = bf16[1,128,6144]{1,2,0:T(8,128)(2,1)S(1)} fusion(bf16[1,128,8,768]{1,3,2,0:T(8,128)(2,1)} %copy.50, f32[6144]{0:T(1024)S(1)} %bitcast.94, f32[128]{0:T(128)S(1)} %broadcast_divide_fusion, pred[128]{0:T(512)(128)(4,1)S(1)} %and_reduce_fusion), kind=kLoop, calls=%fused_computation.5 | loop fusion | flops 3932160 | bytes 3170944 | tf_op jit(solution)/shard_map/jit(_where)/select_n | solution.py:119
  129.3 1.6 %copy.51 = bf16[1,128,6144]{2,1,0:T(8,128)(2,1)} copy(bf16[1,128,6144]{1,2,0:T(8,128)(2,1)S(1)} %fusion.2) | data formatting | bytes 3145728 | tf_op jit(solution)/shard_map/jit(_where)/select_n | solution.py:119
  (30 shorter events, 0.5 us)
Async XLA Ops:
  6.5 3.2 %copy-start = (bf16[256,1024]{1,0:T(8,128)(2,1)S(1)}, bf16[256,1024]{1,0:T(8,128)(2,1)}, u32[]{:S(2)}) copy-start(bf16[256,1024]{1,0:T(8,128)(2,1)} %param.10) | copy-start | bytes 1572868
  6.5 77.8 %all-gather.3.cloned.1.call-start = ((), (), s32[]{:S(2)}) async-start(), calls=%async_computation.1 | async-start | bytes 4718592 | tf_op jit(solution)/shard_map/all_gather | solution.py:88
  9.8 2.6 %copy-start.1 = (bf16[256,1024]{0,1:T(8,128)(2,1)}, bf16[256,1024]{0,1:T(8,128)(2,1)S(1)}, u32[]{:S(2)}) copy-start(bf16[256,1024]{0,1:T(8,128)(2,1)S(1)} %copy.54) | copy-start | bytes 1572868
  12.5 9.1 %collective-permute-start = (bf16[8,128,128]{2,1,0:T(8,128)(2,1)S(1)}, bf16[8,128,128]{2,1,0:T(8,128)(2,1)S(1)}, u32[]{:S(2)}, u32[]{:S(2)}) collective-permute-start(bf16[8,128,128]{2,1,0:T(8,128)(2,1)S(1)} %fusion.48), channel_id=1, source_target_pairs={{0,8},{8,16},{16,24},{1,9},{9,17},{17,25},{2,10},{10,18},{18,26},{... | collective-permute-start | bytes 786440 | tf_op jit(solution)/shard_map/while/body/eval_jaxpr/ppermute | solution.py:15
  21.8 8.1 %collective-permute-start = (bf16[8,128,128]{2,1,0:T(8,128)(2,1)S(1)}, bf16[8,128,128]{2,1,0:T(8,128)(2,1)S(1)}, u32[]{:S(2)}, u32[]{:S(2)}) collective-permute-start(bf16[8,128,128]{2,1,0:T(8,128)(2,1)S(1)} %fusion.48), channel_id=1, source_target_pairs={{0,8},{8,16},{16,24},{1,9},{9,17},{17,25},{2,10},{10,18},{18,26},{... | collective-permute-start | bytes 786440 | tf_op jit(solution)/shard_map/while/body/eval_jaxpr/ppermute | solution.py:15
  30.1 7.1 %collective-permute-start = (bf16[8,128,128]{2,1,0:T(8,128)(2,1)S(1)}, bf16[8,128,128]{2,1,0:T(8,128)(2,1)S(1)}, u32[]{:S(2)}, u32[]{:S(2)}) collective-permute-start(bf16[8,128,128]{2,1,0:T(8,128)(2,1)S(1)} %fusion.48), channel_id=1, source_target_pairs={{0,8},{8,16},{16,24},{1,9},{9,17},{17,25},{2,10},{10,18},{18,26},{... | collective-permute-start | bytes 786440 | tf_op jit(solution)/shard_map/while/body/eval_jaxpr/ppermute | solution.py:15
  39.6 3.5 %copy-start.3 = (s32[256,2]{0,1:T(2,128)S(1)}, s32[256,2]{0,1:T(2,128)}, u32[]{:S(2)}) copy-start(s32[256,2]{0,1:T(2,128)} %param.15) | copy-start | bytes 6148
  95.5 3.9 %copy-start.2 = (f32[768]{0:T(1024)S(1)}, f32[768]{0:T(1024)}, u32[]{:S(2)}) copy-start(f32[768]{0:T(1024)} %param.17) | copy-start | bytes 9220
  95.5 29.3 %copy-start.4 = (s32[64]{0:T(128)S(1)}, s32[64]{0:T(128)}, u32[]{:S(2)}) copy-start(s32[64]{0:T(128)} %param.16) | copy-start | bytes 772
  95.5 29.7 %all-to-all-start = ((bf16[8,128,768]{2,1,0:T(8,128)(2,1)}), bf16[8,128,768]{2,1,0:T(8,128)(2,1)S(1)}, u32[]{:S(2)}, u32[]{:S(2)}) async-start(bf16[8,128,768]{2,1,0:T(8,128)(2,1)} %convolution_convert_fusion), calls=%async_computation | async-start | bytes 3145728 | tf_op jit(solution)/shard_map/all_to_all | solution.py:110
Sparse Core Ops, SparseCore 0:
  43.2 41.0 all-gather.2

commit v2 on v1

--- a/solution.py
+++ b/solution.py
@@ -1,12 +1,17 @@
+import functools
+
 import jax
 import jax.numpy as jnp
 from jax import lax
+from jax.experimental import pallas as pl
+from jax.experimental.pallas import tpu as pltpu
 from jax.sharding import PartitionSpec as P
 
 HEAD = 128
 TOP = 2
 EXP_DEV = 1
 SUB = 256
+MESH = pl.DeviceIdType.MESH
 
 
 def passed_along(value, axis, steps):
@@ -46,6 +51,302 @@
     return (outputs * lax.rsqrt(mean_square + 1e-06)).astype(jnp.bfloat16)
 
 
+def relayed(devices):
+    return devices == 8
+
+
+def exchange_kernel(
+    devices,
+    capacity,
+    own_ref,
+    weight_hbm,
+    slot_ref,
+    flag_ref,
+    direction_ref,
+    out_ref,
+    weight,
+    blocks,
+    total,
+    tiles,
+    landed,
+    directions,
+    weight_sem,
+    block_send,
+    block_recv,
+    tile_send,
+    tile_recv,
+    direction_send,
+    direction_recv,
+):
+    me = lax.axis_index("ep")
+    core = lax.rem(me, 2)
+    sibling = me + 1 - 2 * core
+    rows, width = own_ref.shape
+    half = rows // 2
+    cols = weight.shape[0]
+    pairs = devices // 2
+
+    load = pltpu.make_async_copy(weight_hbm, weight, weight_sem)
+    load.start()
+    barrier = pltpu.get_barrier_semaphore()
+
+    def greet(step, carry):
+        pl.semaphore_signal(
+            barrier, inc=1, device_id={"ep": lax.rem(me + step, devices)}, device_id_type=MESH
+        )
+        return carry
+
+    lax.fori_loop(1, devices, greet, 0)
+    pl.semaphore_wait(barrier, devices - 1)
+
+    sends = []
+
+    def part(ref, side):
+        return ref.at[pl.ds(side * half, half)]
+
+    def send(source, origin, side, target):
+        copy = pltpu.make_async_remote_copy(
+            src_ref=source,
+            dst_ref=part(blocks.at[origin], side),
+            send_sem=block_send.at[len(sends)],
+            recv_sem=block_recv.at[origin, side],
+            device_id={"ep": target},
+            device_id_type=MESH,
+        )
+        copy.start()
+        sends.append(copy)
+
+    def arrived(origin, side):
+        landing = part(blocks.at[origin], side)
+        pltpu.make_async_copy(landing, landing, block_recv.at[origin, side]).wait()
+
+    def forward(origin, side, target):
+        send(part(blocks.at[origin], side), origin, side, target)
+
+    def multiply(origin):
+        columns = pl.ds(pl.multiple_of(origin * width, width), width)
+        total[...] += lax.dot_general(
+            blocks[origin],
+            weight[:, columns],
+            (((1,), (1,)), ((), ())),
+            preferred_element_type=jnp.float32,
+        )
+
+    if relayed(devices):
+        x_bit = lax.rem(me // 2, 2)
+        y_bit = me // 4
+        x_peer = me + 2 - 4 * x_bit
+        y_peer = me + 4 - 8 * y_bit
+        corner = x_peer + 4 - 8 * y_bit
+        send(part(own_ref, 0), me, 0, x_peer)
+        send(part(own_ref, 1), me, 1, y_peer)
+        send(part(own_ref, 1), me, 1, x_peer)
+        send(part(own_ref, 0), me, 0, y_peer)
+    else:
+        for step in range(1, pairs):
+            peer = lax.rem(me + 2 * step, devices)
+            for side in range(2):
+                send(part(own_ref, side), me, side, peer)
+    for side in range(2):
+        send(part(own_ref, side), me, side, sibling)
+
+    def share(step, carry):
+        peer = lax.rem(me + step, devices)
+        pltpu.make_async_remote_copy(
+            src_ref=direction_ref,
+            dst_ref=directions.at[me],
+            send_sem=direction_send.at[step],
+            recv_sem=direction_recv.at[me],
+            device_id={"ep": peer},
+            device_id_type=MESH,
+        ).start()
+        return carry
+
+    lax.fori_loop(1, devices, share, 0)
+    directions[pl.ds(me, 1)] = direction_ref[...][None]
+
+    load.wait()
+    columns = pl.ds(pl.multiple_of(me * width, width), width)
+    total[...] = lax.dot_general(
+        own_ref[...],
+        weight[:, columns],
+        (((1,), (1,)), ((), ())),
+        preferred_element_type=jnp.float32,
+    )
+
+    if relayed(devices):
+        arrived(x_peer, 0)
+        forward(x_peer, 0, y_peer)
+        forward(x_peer, 0, sibling)
+        arrived(y_peer, 1)
+        forward(y_peer, 1, x_peer)
+        forward(y_peer, 1, sibling)
+        arrived(x_peer, 1)
+        forward(x_peer, 1, sibling)
+        arrived(y_peer, 0)
+        forward(y_peer, 0, sibling)
+        arrived(sibling, 0)
+        arrived(sibling, 1)
+
+        def multiply_first(step, carry):
+            origin = jnp.where(step == 0, sibling, jnp.where(step == 1, x_peer, y_peer))
+            multiply(origin)
+            return carry
+
+        lax.fori_loop(0, 3, multiply_first, 0)
+        arrived(corner, 0)
+        forward(corner, 0, sibling)
+        arrived(corner, 1)
+        forward(corner, 1, sibling)
+        multiply(corner)
+        turn = sibling - me
+        for origin in (x_peer, y_peer, corner):
+            arrived(origin + turn, 0)
+            arrived(origin + turn, 1)
+
+        def multiply_last(step, carry):
+            origin = jnp.where(step == 0, x_peer, jnp.where(step == 1, y_peer, corner))
+            multiply(origin + turn)
+            return carry
+
+        lax.fori_loop(0, 3, multiply_last, 0)
+    else:
+        for step in range(1, pairs):
+            origin = lax.rem(me + devices - 2 * step, devices)
+            for side in range(2):
+                arrived(origin, side)
+                forward(origin, side, sibling)
+
+        def multiply_same(step, carry):
+            multiply(lax.rem(me + 2 * step, devices))
+            return carry
+
+        lax.fori_loop(1, pairs, multiply_same, 0)
+
+        def multiply_other(step, carry):
+            origin = lax.rem(sibling + 2 * step, devices)
+            arrived(origin, 0)
+            arrived(origin, 1)
+            multiply(origin)
+            return carry
+
+        lax.fori_loop(0, pairs, multiply_other, 0)
+
+    projected = total[...].astype(jnp.bfloat16)
+    slots = lax.broadcasted_iota(jnp.int32, (capacity, rows), 0)
+
+    def picked(expert):
+        return slot_ref[expert] == slots
+
+    def tile_of(expert):
+        picks = jnp.where(picked(expert), 1.0, 0.0).astype(jnp.bfloat16)
+        return jnp.dot(picks, projected, preferred_element_type=jnp.float32).astype(jnp.bfloat16)
+
+    def tile_copy(expert):
+        return pltpu.make_async_remote_copy(
+            src_ref=tiles.at[expert],
+            dst_ref=landed.at[me],
+            send_sem=tile_send.at[expert],
+            recv_sem=tile_recv.at[me],
+            device_id={"ep": expert},
+            device_id_type=MESH,
+        )
+
+    def dispatch(step, carry):
+        expert = lax.rem(me + step, devices)
+        tiles[expert] = tile_of(expert)
+        tile_copy(expert).start()
+        return carry
+
+    lax.fori_loop(1, devices, dispatch, 0)
+    landed[me] = tile_of(me)
+    flags = jnp.sum(jnp.where(picked(me), flag_ref[...], 0.0), axis=1, keepdims=True) > 0.5
+
+    def direction_wait(step, carry):
+        origin = lax.rem(me + step, devices)
+        landing = directions.at[origin]
+        pltpu.make_async_copy(landing, landing, direction_recv.at[origin]).wait()
+        return carry
+
+    lax.fori_loop(1, devices, direction_wait, 0)
+    squares = jnp.sum(directions[...] * directions[...], axis=0)
+    norm_square = jnp.sum(squares, axis=1, keepdims=True) + 1e-06
+
+    def product(origin):
+        return jnp.sum(
+            landed[origin].astype(jnp.float32) * directions[origin], axis=1, keepdims=True
+        )
+
+    def tile_wait(step, products):
+        origin = lax.rem(me + step, devices)
+        landing = landed.at[origin]
+        pltpu.make_async_copy(landing, landing, tile_recv.at[origin]).wait()
+        return products + product(origin)
+
+    products = lax.fori_loop(1, devices, tile_wait, product(me))
+    gain = products / norm_square
+
+    def finish(origin, carry):
+        tile = landed[origin]
+        removed = (tile.astype(jnp.float32) - gain * directions[origin]).astype(jnp.bfloat16)
+        result = jnp.where(flags, removed, tile)
+        if cols % 128:
+            out_ref[origin] = result
+        else:
+            out_ref[:, pl.ds(pl.multiple_of(origin * cols, cols), cols)] = result
+        return carry
+
+    lax.fori_loop(0, devices, finish, 0)
+
+    for copy in sends:
+        copy.wait_send()
+
+    def sent(step, carry):
+        expert = lax.rem(me + step, devices)
+        tile_copy(expert).wait_send()
+        pltpu.make_async_copy(direction_ref, direction_ref, direction_send.at[step]).wait()
+        return carry
+
+    lax.fori_loop(1, devices, sent, 0)
+
+
+def project_and_dispatch(attended, out_weight, slot_index, row_flags, direction, capacity):
+    devices = lax.axis_size("ep")
+    rows, width = attended.shape
+    cols = out_weight.shape[0]
+    copies = 16 if relayed(devices) else 4 * devices
+    shape = (devices, capacity, cols) if cols % 128 else (capacity, devices * cols)
+    vmem = pl.BlockSpec(memory_space=pltpu.VMEM)
+    return pl.pallas_call(
+        functools.partial(exchange_kernel, devices, capacity),
+        out_shape=jax.ShapeDtypeStruct(shape, jnp.bfloat16),
+        in_specs=[vmem, pl.BlockSpec(memory_space=pl.ANY), vmem, vmem, vmem],
+        out_specs=vmem,
+        scratch_shapes=[
+            pltpu.VMEM(out_weight.shape, jnp.bfloat16),
+            pltpu.VMEM((devices, rows, width), jnp.bfloat16),
+            pltpu.VMEM((rows, cols), jnp.float32),
+            pltpu.VMEM((devices, capacity, cols), jnp.bfloat16),
+            pltpu.VMEM((devices, capacity, cols), jnp.bfloat16),
+            pltpu.VMEM((devices, 1, cols), jnp.float32),
+            pltpu.SemaphoreType.DMA,
+            pltpu.SemaphoreType.DMA((copies,)),
+            pltpu.SemaphoreType.DMA((devices, 2)),
+            pltpu.SemaphoreType.DMA((devices,)),
+            pltpu.SemaphoreType.DMA((devices,)),
+            pltpu.SemaphoreType.DMA((devices,)),
+            pltpu.SemaphoreType.DMA((devices,)),
+        ],
+        compiler_params=pltpu.CompilerParams(
+            collective_id=0, has_side_effects=True, vmem_limit_bytes=40 * 1024 * 1024
+        ),
+        cost_estimate=pl.CostEstimate(
+            flops=2 * rows * devices * width * cols, bytes_accessed=out_weight.size * 2,
+            transcendentals=0,
+        ),
+    )(attended, out_weight, slot_index, row_flags, direction)
+
+
 def local(queries, key_rows, value_rows, log_decay, out_weight, expert_ids, flagged, direction):
     block_rows = queries.shape[0]
     local_width = queries.shape[1]
@@ -84,12 +385,6 @@
         "cthd,hde->cthe", scaled, incoming, precision=lax.Precision.HIGHEST
     )
     attended = normalize(outputs).reshape(block_rows, local_width)
-    projected = lax.dot_general(
-        lax.all_gather(attended, "ep", axis=1, tiled=True),
-        out_weight,
-        (((1,), (1,)), ((), ())),
-        preferred_element_type=jnp.float32,
-    ).astype(jnp.bfloat16)
     ctx_start = lax.axis_index("ctx") * block_rows
     local_flags = flagged - ctx_start
     experts_all = lax.axis_size("ep") * EXP_DEV
@@ -99,24 +394,19 @@
     named = jnp.any(expert_ids[:, :, None] == expert_number[None, None, :], axis=1)
     before = (row_number[:, None] > row_number[None, :]).astype(jnp.bfloat16)
     slot_index = jnp.dot(before, named.astype(jnp.bfloat16), preferred_element_type=jnp.float32)
-    slot_index = jnp.where(named, slot_index.astype(jnp.int32), -1).T
-    picks = slot_index[:, None, :] == jnp.arange(capacity, dtype=jnp.int32)[None, :, None]
-    tile_rows = jnp.einsum(
-        "ecr,rm->ecm",
-        picks.astype(jnp.bfloat16),
-        projected,
-        preferred_element_type=jnp.float32,
-    ).astype(jnp.bfloat16)
-    tiles = lax.all_to_all(tile_rows, "ep", split_axis=0, concat_axis=2, tiled=True)
-    row_flags = jnp.any(local_flags[:, None] == row_number[None, :], axis=0)
-    own_picks = lax.dynamic_slice_in_dim(picks, lax.axis_index("ep") * EXP_DEV, EXP_DEV, 0)
-    slot_flags = jnp.any(own_picks & row_flags[None, None, :], axis=2)
-    whole_direction = lax.all_gather(direction, "ep", tiled=True)
-    norm_square = jnp.sum(whole_direction * whole_direction) + 1e-06
-    rows = tiles.astype(jnp.float32)
-    products = jnp.sum(rows * whole_direction, axis=2)
-    removed = rows - (products / norm_square)[:, :, None] * whole_direction
-    return jnp.where(slot_flags[:, :, None], removed.astype(jnp.bfloat16), tiles)
+    slot_index = jnp.where(named, slot_index.astype(jnp.int32), -1).T[:, None, :]
+    row_flags = jnp.any(local_flags[:, None] == row_number[None, :], axis=0, keepdims=True)
+    tiles = project_and_dispatch(
+        attended,
+        out_weight,
+        slot_index,
+        row_flags.astype(jnp.float32),
+        direction[None, :],
+        capacity,
+    )
+    if tiles.ndim == 3:
+        tiles = jnp.transpose(tiles, (1, 0, 2)).reshape(capacity, -1)
+    return tiles[None]
 
 
 def solution(mesh):

time: 139 us -> 89 us (0.64)
  Pallas kernels: 0 us -> 49.1 us
  waiting for transfers between devices: 61.5 us -> 20.4 us
  blocking collectives: 24 us -> 0 us
  between operations: 14.2 us -> 0.11 us
  matrix products: 18.8 us -> 7.46 us
  starting transfers between devices: 7.74 us -> 3.88 us
  other arithmetic: 6.58 us -> 3.69 us
    pallas_call x0 -> x1, Pallas kernels: none -> 49.1 us  [project_and_dispatch(): pl.pallas_call(functools.partial(exchange_kernel, devices, capacity), out...]
    all_gather x1 -> x0, waiting for transfers between devices: 41 us -> none  [local(): lax.all_gather(attended, 'ep', axis=1, tiled=True)]
    all_gather x1 -> x0, blocking collectives: 24 us -> none  [local(): whole_direction = lax.all_gather(direction, 'ep', tiled=True)]
    dot_general x1 -> x0, matrix products: 11.2 us -> none  [local(): jnp.einsum('ecr,rm->ecm', picks.astype(jnp.bfloat16), projected, preferre...]
    all_to_all x1 -> x0, starting transfers between devices: 3.86 us -> none  [local(): lax.all_to_all(tile_rows, 'ep', split_axis=0, concat_axis=2, tiled=True)]
    select_n x1 -> x0, other arithmetic: 2.12 us -> none  [local(): jnp.where(slot_flags[:, :, None], removed.astype(jnp.bfloat16), tiles)]
    select_n x1 -> x0, local copies, waits for them, and re-layouts: 1.57 us -> none  [local(): jnp.where(slot_flags[:, :, None], removed.astype(jnp.bfloat16), tiles)]
    all_to_all x1 -> x0, local copies, waits for them, and re-layouts: 1.57 us -> none  [local(): lax.all_to_all(tile_rows, 'ep', split_axis=0, concat_axis=2, tiled=True)]
  transfers between devices with their start and end apart: 5 -> 3, of which waited for: 4 -> 3; matrix products, arithmetic and copies ran while one was open for 1% -> 0% of each run, Pallas kernels for 0% -> 0%
where the time goes in v2:
time: 89 us; the launch traced here: 88.4 us
  Pallas kernels  49.1 us (55%)
  waiting for transfers between devices  20.4 us (23%)
  matrix products  7.46 us (8%)
  starting transfers between devices  3.88 us (4%)
  other arithmetic  3.69 us (4%)
  local copies, waits for them, and re-layouts  3.67 us (4%)
    pallas_call x1, Pallas kernels, project_and_dispatch(): pl.pallas_call(functools.partial(exchange_kernel, devices, capacity), out...  49.1 us
    ppermute x3, waiting for transfers between devices, passed_along(): lax.ppermute(value, axis, [(source, source + steps) for source in range(l...  20.4 us
    ppermute x3, starting transfers between devices, passed_along(): lax.ppermute(value, axis, [(source, source + steps) for source in range(l...  3.88 us
    dot_general x1, matrix products, local(): jnp.einsum('cthd,hde->cthe', scaled, incoming, precision=lax.Precision.HI...  2.37 us
    dot_general x1, matrix products, local_step(): jnp.einsum('hts,shd->thd', weights, value_sub, preferred_element_type=jnp...  2.35 us
  transfers between devices with their start and end apart: 3, of which 3 were waited for; matrix products, arithmetic and copies ran while one was open for 0% of the time, Pallas kernels for 0%

profile of v2, /device:TPU:25, one launch (start us, length us, event | category | flops | bytes accessed | tf_op | source)
XLA Modules:
  0.0 88.4 jit_solution(7835869632324812233)
XLA Ops:
  0.0 0.0 copy-start
  0.0 0.7 broadcast_subtract_fusion
  0.7 0.1 fusion.28
  0.8 0.7 fusion.29
  1.5 0.7 broadcast_in_dim.68.direction_ref
  2.2 0.2 fusion.7
  2.4 1.3 %reduce-window.6 = f32[8,2,128]{2,0,1:T(8,128)S(1)} reduce-window(f32[8,2,128]{2,0,1:T(8,128)} %bitcast.80, f32[]{:T(128)} %constant.16.clone.1), window={size=1x1x128 pad=0_0x0_0x127_0}, to_apply=%region_0.1 | reduce-window | flops 260096 | bytes 16388 | tf_op jit(solution)/shard_map/reduce-window
  3.7 0.2 slice_reduce_fusion
  3.9 0.1 add_bitcast_fusion.1
  3.9 0.1 fusion.32
  4.0 0.2 slice_reduce_fusion.1
  4.2 0.1 subtract_exponential_fusion
  4.3 1.2 %copy.42 = bf16[256,1024]{0,1:T(8,128)(2,1)S(1)} copy(bf16[256,1024]{1,0:T(8,128)(2,1)} %param.11) | data formatting | bytes 1048576 | tf_op jit(solution)/shard_map/while/body/jit(dynamic_index_in_dim)/squeeze | solution.py:364
  5.6 1.3 %convolution_add_fusion = f32[8,128,128]{2,1,0:T(8,128)S(1)} fusion(bf16[256,8,128]{0,2,1:T(8,128)(2,1)S(1)} %bitcast.78, f32[256,8]{0,1:T(8,128)S(1)} %subtract_exponential_fusion, f32[8]{0:T(128)S(1)} %get-tuple-element.80, bf16[256,1024]{1,0:T(8,128)(2,1)} %param.12), kind=kOutput, calls=%fused_computation.11 | convolution fusion | flops 68026368 | bytes 1581088 | tf_op jit(solution)/shard_map/while/body/eval_jaxpr/shd,she->hde/dot_general | solution.py:43
  6.9 24.9 %while.3 = (s32[]{:T(128)}, f32[8,128,128]{2,1,0:T(8,128)S(1)}, f32[8]{0:T(128)S(1)}, f32[8,128,128]{2,1,0:T(8,128)S(1)}, s32[]{:T(128)}, /*index=5*/s32[]{:T(128)}) while((s32[]{:T(128)}, f32[8,128,128]{2,1,0:T(8,128)S(1)}, f32[8]{0:T(128)S(1)}, f32[8,128,128]{2,1,0:T(8,128)S(1)}, s32[]{:T(128)}, /*index=5*/s32[]{:T(128)}) %tuple.27), condition=%wide.region_3.4_spmd.clone, body=%wide.region_2.3_spmd.clone.sunk | while | flops 655363 | bytes 3145879 | solution.py:382
  6.9 0.1 fusion.44
  7.1 1.3 %collective-permute-start = (bf16[8,128,128]{2,1,0:T(8,128)(2,1)S(1)}, bf16[8,128,128]{2,1,0:T(8,128)(2,1)S(1)}, u32[]{:S(2)}, u32[]{:S(2)}) collective-permute-start(bf16[8,128,128]{2,1,0:T(8,128)(2,1)S(1)} %fusion.44), channel_id=1, source_target_pairs={{0,8},{8,16},{16,24},{1,9},{9,17},{17,25},{2,10},{10,18},{18,26},{... | collective-permute-start | bytes 786440 | tf_op jit(solution)/shard_map/while/body/eval_jaxpr/ppermute | solution.py:20
  8.4 7.8 %collective-permute-done = bf16[8,128,128]{2,1,0:T(8,128)(2,1)S(1)} collective-permute-done((bf16[8,128,128]{2,1,0:T(8,128)(2,1)S(1)}, bf16[8,128,128]{2,1,0:T(8,128)(2,1)S(1)}, u32[]{:S(2)}, u32[]{:S(2)}) %collective-permute-start) | collective-permute-done | bytes 262176 | tf_op jit(solution)/shard_map/while/body/eval_jaxpr/ppermute | solution.py:20
  16.2 0.1 fusion.44
  16.3 1.3 %collective-permute-start = (bf16[8,128,128]{2,1,0:T(8,128)(2,1)S(1)}, bf16[8,128,128]{2,1,0:T(8,128)(2,1)S(1)}, u32[]{:S(2)}, u32[]{:S(2)}) collective-permute-start(bf16[8,128,128]{2,1,0:T(8,128)(2,1)S(1)} %fusion.44), channel_id=1, source_target_pairs={{0,8},{8,16},{16,24},{1,9},{9,17},{17,25},{2,10},{10,18},{18,26},{... | collective-permute-start | bytes 786440 | tf_op jit(solution)/shard_map/while/body/eval_jaxpr/ppermute | solution.py:20
  17.6 6.8 %collective-permute-done = bf16[8,128,128]{2,1,0:T(8,128)(2,1)S(1)} collective-permute-done((bf16[8,128,128]{2,1,0:T(8,128)(2,1)S(1)}, bf16[8,128,128]{2,1,0:T(8,128)(2,1)S(1)}, u32[]{:S(2)}, u32[]{:S(2)}) %collective-permute-start) | collective-permute-done | bytes 262176 | tf_op jit(solution)/shard_map/while/body/eval_jaxpr/ppermute | solution.py:20
  24.5 0.1 fusion.44
  24.7 1.3 %collective-permute-start = (bf16[8,128,128]{2,1,0:T(8,128)(2,1)S(1)}, bf16[8,128,128]{2,1,0:T(8,128)(2,1)S(1)}, u32[]{:S(2)}, u32[]{:S(2)}) collective-permute-start(bf16[8,128,128]{2,1,0:T(8,128)(2,1)S(1)} %fusion.44), channel_id=1, source_target_pairs={{0,8},{8,16},{16,24},{1,9},{9,17},{17,25},{2,10},{10,18},{18,26},{... | collective-permute-start | bytes 786440 | tf_op jit(solution)/shard_map/while/body/eval_jaxpr/ppermute | solution.py:20
  26.0 5.8 %collective-permute-done = bf16[8,128,128]{2,1,0:T(8,128)(2,1)S(1)} collective-permute-done((bf16[8,128,128]{2,1,0:T(8,128)(2,1)S(1)}, bf16[8,128,128]{2,1,0:T(8,128)(2,1)S(1)}, u32[]{:S(2)}, u32[]{:S(2)}) %collective-permute-start) | collective-permute-done | bytes 262176 | tf_op jit(solution)/shard_map/while/body/eval_jaxpr/ppermute | solution.py:20
  31.9 0.0 copy-done
  31.9 2.4 %convolution_bitcast_fusion = f32[1,256,8,128]{1,3,2,0:T(8,128)} fusion(f32[8,128,128]{2,1,0:T(8,128)S(1)} %get-tuple-element.52, f32[256,8]{0,1:T(8,128)S(1)} %get-tuple-element.78, bf16[256,1024]{1,0:T(8,128)(2,1)S(1)} %copy-done), kind=kOutput, calls=%fused_computation.8 | convolution fusion | flops 403177472 | bytes 2105344 | tf_op jit(solution)/shard_map/cthd,hde->cthe/dot_general | solution.py:384
  34.2 1.2 %convolution_bitcast_fusion.1 = f32[256,8,128]{0,2,1:T(8,128)S(1)} fusion(f32[256,8]{0,1:T(8,128)S(1)} %get-tuple-element.78, bf16[256,1024]{1,0:T(8,128)(2,1)S(1)} %copy-done), kind=kOutput, calls=%fused_computation.9 | convolution fusion | flops 403177472 | bytes 1581056 | tf_op jit(solution)/shard_map/while/body/eval_jaxpr/thd,hde->the/dot_general | solution.py:38
  35.5 2.4 %multiply_reduce_fusion = (f32[256,8]{0,1:T(8,128)S(1)}, f32[1,256,8,128]{1,3,2,0:T(8,128)S(1)}) fusion(f32[1,256,8,128]{1,3,2,0:T(8,128)} %convolution_bitcast_fusion, f32[256,8,128]{0,2,1:T(8,128)S(1)} %convolution_bitcast_fusion.1, bf16[256,8,128]{0,2,1:T(8,128)(2,1)S(1)} %bitcast.79, f32[8,256]{1,0:T(8,128)S(1)} %add_bitcast_fusion.1, ...), kind=kOutput, calls=%fused_computation.15 | convolution fusion | flops 272103424 | bytes 4800512 | tf_op jit(solution)/shard_map/while/body/eval_jaxpr/hts,shd->thd/dot_general | solution.py:36
  37.9 0.1 multiply_convert_fusion
  38.0 0.2 copy.41.own_ref
  38.2 49.1 %shard_map.82 = bf16[128,6144]{1,0:T(8,128)(2,1)S(1)} custom-call(bf16[256,1024]{1,0:T(8,128)(2,1)S(1)} %copy.41.own_ref, bf16[768,8192]{1,0:T(8,128)(2,1)} %weight_hbm.1, s32[8,1,256]{2,1,0:T(1,128)S(1)} %broadcast_in_dim.67.slot_ref, f32[1,256]{1,0:T(1,128)S(1)} %bitcast.76, f32[1,768]{1,0:T(1,128)S(1)} %broadcast_in_dim.68.direction_ref), custom_call_target="tpu_custom_call" | custom-call | flops 3221225472 | bytes 12582912 | tf_op jit(solution)/shard_map/pallas_call | solution.py:320
  87.3 1.1 %copy.77 = bf16[1,128,6144]{2,1,0:T(8,128)(2,1)} copy(bf16[1,128,6144]{2,1,0:T(8,128)(2,1)S(1)} %bitcast.75) | data formatting | bytes 3145728
  (11 shorter events, 0.2 us)
Async XLA Ops:
  0.0 31.9 %copy-start = (bf16[256,1024]{1,0:T(8,128)(2,1)S(1)}, bf16[256,1024]{1,0:T(8,128)(2,1)}, u32[]{:S(2)}) copy-start(bf16[256,1024]{1,0:T(8,128)(2,1)} %param.10) | copy-start | bytes 1572868
  7.1 9.1 %collective-permute-start = (bf16[8,128,128]{2,1,0:T(8,128)(2,1)S(1)}, bf16[8,128,128]{2,1,0:T(8,128)(2,1)S(1)}, u32[]{:S(2)}, u32[]{:S(2)}) collective-permute-start(bf16[8,128,128]{2,1,0:T(8,128)(2,1)S(1)} %fusion.44), channel_id=1, source_target_pairs={{0,8},{8,16},{16,24},{1,9},{9,17},{17,25},{2,10},{10,18},{18,26},{... | collective-permute-start | bytes 786440 | tf_op jit(solution)/shard_map/while/body/eval_jaxpr/ppermute | solution.py:20
  16.3 8.1 %collective-permute-start = (bf16[8,128,128]{2,1,0:T(8,128)(2,1)S(1)}, bf16[8,128,128]{2,1,0:T(8,128)(2,1)S(1)}, u32[]{:S(2)}, u32[]{:S(2)}) collective-permute-start(bf16[8,128,128]{2,1,0:T(8,128)(2,1)S(1)} %fusion.44), channel_id=1, source_target_pairs={{0,8},{8,16},{16,24},{1,9},{9,17},{17,25},{2,10},{10,18},{18,26},{... | collective-permute-start | bytes 786440 | tf_op jit(solution)/shard_map/while/body/eval_jaxpr/ppermute | solution.py:20
  24.7 7.1 %collective-permute-start = (bf16[8,128,128]{2,1,0:T(8,128)(2,1)S(1)}, bf16[8,128,128]{2,1,0:T(8,128)(2,1)S(1)}, u32[]{:S(2)}, u32[]{:S(2)}) collective-permute-start(bf16[8,128,128]{2,1,0:T(8,128)(2,1)S(1)} %fusion.44), channel_id=1, source_target_pairs={{0,8},{8,16},{16,24},{1,9},{9,17},{17,25},{2,10},{10,18},{18,26},{... | collective-permute-start | bytes 786440 | tf_op jit(solution)/shard_map/while/body/eval_jaxpr/ppermute | solution.py:20

commit v3 on v1

v3 whole, which is shorter than its diff:
```python
import functools

import jax
import jax.numpy as jnp
from jax import lax
from jax.experimental import pallas as pl
from jax.experimental.pallas import tpu as pltpu
from jax.sharding import PartitionSpec as P

HEAD = 128
TOP = 2
EXP_DEV = 1
SUB = 256
MESH = pl.DeviceIdType.MESH


def relayed(devices):
    return devices == 8


def layer_kernel(
    devices,
    blocks_of_sequence,
    capacity,
    query_ref,
    key_ref,
    value_ref,
    decay_ref,
    weight_hbm,
    slot_ref,
    flag_ref,
    direction_ref,
    out_ref,
    weight,
    cumulated,
    cumulated_rows,
    incoming,
    outgoing,
    attended,
    gathered,
    total,
    projected,
    spread_out,
    tiles,
    products,
    directions,
    weight_sem,
    state_send,
    state_recv,
    block_send,
    block_recv,
    row_send,
    row_recv,
    direction_send,
    direction_recv,
):
    me = lax.axis_index("ep")
    place = lax.axis_index("ctx")
    core = lax.rem(me, 2)
    turn = 1 - 2 * core
    sibling = me + turn
    rows, width = query_ref.shape
    heads = width // HEAD
    cols = weight.shape[0]
    pairs = devices // 2
    has_next = place < blocks_of_sequence - 1

    load = pltpu.make_async_copy(weight_hbm, weight, weight_sem)
    load.start()
    barrier = pltpu.get_barrier_semaphore()

    def greet(step, carry):
        pl.semaphore_signal(
            barrier, inc=1, device_id={"ep": lax.rem(me + step, devices)}, device_id_type=MESH
        )
        return carry

    lax.fori_loop(1, devices, greet, 0)

    @pl.when(place > 0)
    def _():
        pl.semaphore_signal(barrier, inc=1, device_id={"ctx": place - 1}, device_id_type=MESH)

    t_index = lax.broadcasted_iota(jnp.int32, (rows, rows), 0)
    s_index = lax.broadcasted_iota(jnp.int32, (rows, rows), 1)
    causal = t_index >= s_index
    lower = jnp.where(causal, 1.0, 0.0)
    cumulated[...] = jnp.dot(
        lower,
        decay_ref[...],
        precision=lax.Precision.HIGHEST,
        preferred_element_type=jnp.float32,
    )
    whole_rows = jnp.transpose(cumulated[...])
    for head in range(heads):
        cumulated_rows[head] = whole_rows[head : head + 1, :]

    pl.semaphore_wait(barrier, devices - 1 + jnp.where(has_next, 1, 0))

    def share(step, carry):
        pltpu.make_async_remote_copy(
            src_ref=direction_ref,
            dst_ref=directions.at[me],
            send_sem=direction_send.at[step],
            recv_sem=direction_recv.at[me],
            device_id={"ep": lax.rem(me + step, devices)},
            device_id_type=MESH,
        ).start()
        return carry

    lax.fori_loop(1, devices, share, 0)
    directions[pl.ds(me, 1)] = direction_ref[...][None]

    def state_copy(head):
        return pltpu.make_async_remote_copy(
            src_ref=outgoing.at[head],
            dst_ref=incoming.at[head],
            send_sem=state_send.at[head],
            recv_sem=state_recv.at[head],
            device_id={"ctx": place + 1},
            device_id_type=MESH,
        )

    head_lane = lax.broadcasted_iota(jnp.int32, (rows, heads), 1)

    def attend(side, step, carry):
        head = side * (heads // 2) + step
        columns = pl.ds(pl.multiple_of(head * HEAD, HEAD), HEAD)
        query, key, value = query_ref[:, columns], key_ref[:, columns], value_ref[:, columns]
        level = jnp.sum(
            jnp.where(head_lane == head, cumulated[...], 0.0), axis=1, keepdims=True
        )
        last = level[rows - 1 :, :]
        key_scaled = (key.astype(jnp.float32) * jnp.exp(last - level)).astype(jnp.bfloat16)
        state = lax.dot_general(
            key_scaled, value, (((0,), (0,)), ((), ())), preferred_element_type=jnp.float32
        )
        scores = lax.dot_general(
            query, key, (((1,), (1,)), ((), ())), preferred_element_type=jnp.float32
        )
        gaps = jnp.minimum(level - cumulated_rows[head], 0.0)
        weights = jnp.where(causal, scores * jnp.exp(gaps), 0.0).astype(jnp.bfloat16)
        inside = jnp.dot(weights, value, preferred_element_type=jnp.float32)

        @pl.when(place == 0)
        def _():
            incoming[head] = jnp.zeros((HEAD, HEAD), jnp.bfloat16)

        @pl.when(place > 0)
        def _():
            landing = incoming.at[head]
            pltpu.make_async_copy(landing, landing, state_recv.at[head]).wait()

        before = incoming[head]

        @pl.when(has_next)
        def _():
            outgoing[head] = (jnp.exp(last) * before.astype(jnp.float32) + state).astype(
                jnp.bfloat16
            )
            state_copy(head).start()

        carried = jnp.dot(query, before, preferred_element_type=jnp.float32)
        outputs = inside + jnp.exp(level) * carried
        mean_square = jnp.mean(outputs * outputs, axis=1, keepdims=True)
        own = pl.ds(pl.multiple_of(step * HEAD, HEAD), HEAD)
        attended[side, :, own] = (outputs * lax.rsqrt(mean_square + 1e-06)).astype(jnp.bfloat16)
        return carry

    sends = []
    if relayed(devices):
        x_peer = me + 2 - 4 * lax.rem(me // 2, 2)
        y_peer = me + 4 - 8 * (me // 4)
        corner = x_peer + y_peer - me

    def exchange(own, buffer, send_sem, recv_sem):
        count = []

        def send(source, origin, side, target):
            copy = pltpu.make_async_remote_copy(
                src_ref=source,
                dst_ref=buffer.at[origin, side],
                send_sem=send_sem.at[len(count)],
                recv_sem=recv_sem.at[origin, side],
                device_id={"ep": target},
                device_id_type=MESH,
            )
            copy.start()
            count.append(copy)
            sends.append(copy)

        def arrived(origin, side):
            landing = buffer.at[origin, side]
            pltpu.make_async_copy(landing, landing, recv_sem.at[origin, side]).wait()

        def forward(origin, side, target):
            send(buffer.at[origin, side], origin, side, target)

        def begin(side):
            if relayed(devices):
                peers = (x_peer, y_peer) if side == 0 else (y_peer, x_peer)
            else:
                peers = [lax.rem(me + 2 * step, devices) for step in range(1, pairs)]
            for peer in peers:
                send(own.at[side], me, side, peer)
            send(own.at[side], me, side, sibling)

        def take(use):
            if relayed(devices):
                arrived(x_peer, 0)
                forward(x_peer, 0, y_peer)
                forward(x_peer, 0, sibling)
                arrived(y_peer, 0)
                forward(y_peer, 0, sibling)
                arrived(y_peer, 1)
                forward(y_peer, 1, x_peer)
                forward(y_peer, 1, sibling)
                arrived(x_peer, 1)
                forward(x_peer, 1, sibling)
                arrived(sibling, 0)
                arrived(sibling, 1)

                def use_first(step, carry):
                    use(jnp.where(step == 0, sibling, jnp.where(step == 1, x_peer, y_peer)))
                    return carry

                lax.fori_loop(0, 3, use_first, 0)
                for origin in (x_peer, y_peer):
                    arrived(origin + turn, 0)
                    arrived(origin + turn, 1)

                def use_second(step, carry):
                    use(jnp.where(step == 0, x_peer, y_peer) + turn)
                    return carry

                arrived(corner, 0)
                forward(corner, 0, sibling)
                lax.fori_loop(0, 2, use_second, 0)
                arrived(corner, 1)
                forward(corner, 1, sibling)

                def use_last(step, carry):
                    origin = corner + turn * step
                    for side in range(2):
                        @pl.when(step == 1)
                        def _():
                            arrived(origin, side)
                    use(origin)
                    return carry

                lax.fori_loop(0, 2, use_last, 0)
            else:
                for step in range(1, pairs):
                    origin = lax.rem(me + devices - 2 * step, devices)
                    for side in range(2):
                        arrived(origin, side)
                        forward(origin, side, sibling)

                def use_same(step, carry):
                    use(lax.rem(me + 2 * step, devices))
                    return carry

                lax.fori_loop(1, pairs, use_same, 0)

                def use_other(step, carry):
                    origin = lax.rem(sibling + 2 * step, devices)
                    arrived(origin, 0)
                    arrived(origin, 1)
                    use(origin)
                    return carry

                lax.fori_loop(0, pairs, use_other, 0)

        return begin, take

    begin, take = exchange(attended, gathered, block_send, block_recv)
    for side in range(2):
        lax.fori_loop(0, heads // 2, functools.partial(attend, side), 0)
        begin(side)

    half = width // 2

    def multiplied(block, origin):
        result = None
        for side in range(2):
            columns = pl.ds(pl.multiple_of(origin * width + side * half, half), half)
            term = lax.dot_general(
                block[side],
                weight[:, columns],
                (((1,), (1,)), ((), ())),
                preferred_element_type=jnp.float32,
            )
            result = term if result is None else result + term
        return result

    load.wait()
    total[...] = multiplied(attended, me)

    def multiply(origin):
        total[...] += multiplied(gathered.at[origin], origin)

    take(multiply)

    begin, take = exchange(projected, spread_out, row_send, row_recv)
    part = rows // 2
    for side in range(2):
        projected[side] = total[side * part : (side + 1) * part, :].astype(jnp.bfloat16)
        begin(side)

    slots = lax.broadcasted_iota(jnp.int32, (capacity, rows), 0)
    picked = slot_ref[me] == slots
    picks = jnp.where(picked, 1.0, 0.0).astype(jnp.bfloat16)
    flags = jnp.sum(jnp.where(picked, flag_ref[...], 0.0), axis=1, keepdims=True) > 0.5

    def direction_wait(step, carry):
        origin = lax.rem(me + step, devices)
        landing = directions.at[origin]
        pltpu.make_async_copy(landing, landing, direction_recv.at[origin]).wait()
        return carry

    lax.fori_loop(1, devices, direction_wait, 0)
    squares = jnp.sum(directions[...] * directions[...], axis=0)
    norm_square = jnp.sum(squares, axis=1, keepdims=True) + 1e-06

    def pick(block, origin):
        picked_rows = jnp.dot(
            picks[:, :part], block[0], preferred_element_type=jnp.float32
        ) + jnp.dot(picks[:, part:], block[1], preferred_element_type=jnp.float32)
        tiles[origin] = picked_rows.astype(jnp.bfloat16)
        return jnp.sum(picked_rows * directions[origin], axis=1, keepdims=True)

    products[...] = pick(projected, me)

    def collect(origin):
        products[...] += pick(spread_out.at[origin], origin)

    take(collect)
    gain = products[...] / norm_square

    def finish(origin, carry):
        tile = tiles[origin]
        removed = (tile.astype(jnp.float32) - gain * directions[origin]).astype(jnp.bfloat16)
        result = jnp.where(flags, removed, tile)
        if cols % 128:
            out_ref[origin] = result
        else:
            out_ref[:, pl.ds(pl.multiple_of(origin * cols, cols), cols)] = result
        return carry

    lax.fori_loop(0, devices, finish, 0)

    for copy in sends:
        copy.wait_send()

    @pl.when(has_next)
    def _():
        def state_sent(head, carry):
            state_copy(head).wait_send()
            return carry

        lax.fori_loop(0, heads, state_sent, 0)

    def sent(step, carry):
        pltpu.make_async_copy(direction_ref, direction_ref, direction_send.at[step]).wait()
        return carry

    lax.fori_loop(1, devices, sent, 0)


def layer(
    queries, key_rows, value_rows, log_decay, out_weight, slot_index, row_flags, direction, capacity
):
    devices = lax.axis_size("ep")
    rows, width = queries.shape
    heads = width // HEAD
    cols = out_weight.shape[0]
    copies = 16 if relayed(devices) else 2 * devices
    shape = (devices, capacity, cols) if cols % 128 else (capacity, devices * cols)
    vmem = pl.BlockSpec(memory_space=pltpu.VMEM)
    dma = pltpu.SemaphoreType.DMA
    return pl.pallas_call(
        functools.partial(layer_kernel, devices, lax.axis_size("ctx"), capacity),
        out_shape=jax.ShapeDtypeStruct(shape, jnp.bfloat16),
        in_specs=[vmem] * 4 + [pl.BlockSpec(memory_space=pl.ANY)] + [vmem] * 3,
        out_specs=vmem,
        scratch_shapes=[
            pltpu.VMEM(out_weight.shape, jnp.bfloat16),
            pltpu.VMEM((rows, heads), jnp.float32),
            pltpu.VMEM((heads, 1, rows), jnp.float32),
            pltpu.VMEM((heads, HEAD, HEAD), jnp.bfloat16),
            pltpu.VMEM((heads, HEAD, HEAD), jnp.bfloat16),
            pltpu.VMEM((2, rows, width // 2), jnp.bfloat16),
            pltpu.VMEM((devices, 2, rows, width // 2), jnp.bfloat16),
            pltpu.VMEM((rows, cols), jnp.float32),
            pltpu.VMEM((2, rows // 2, cols), jnp.bfloat16),
            pltpu.VMEM((devices, 2, rows // 2, cols), jnp.bfloat16),
            pltpu.VMEM((devices, capacity, cols), jnp.bfloat16),
            pltpu.VMEM((capacity, 1), jnp.float32),
            pltpu.VMEM((devices, 1, cols), jnp.float32),
            dma,
            dma((heads,)),
            dma((heads,)),
            dma((copies,)),
            dma((devices, 2)),
            dma((copies,)),
            dma((devices, 2)),
            dma((devices,)),
            dma((devices,)),
        ],
        compiler_params=pltpu.CompilerParams(
            collective_id=0, has_side_effects=True, vmem_limit_bytes=44 * 1024 * 1024
        ),
        cost_estimate=pl.CostEstimate(
            flops=2 * rows * devices * width * cols, bytes_accessed=out_weight.size * 2,
            transcendentals=0,
        ),
    )(queries, key_rows, value_rows, log_decay, out_weight, slot_index, row_flags, direction)


def local(queries, key_rows, value_rows, log_decay, out_weight, expert_ids, flagged, direction):
    block_rows = queries.shape[0]
    assert block_rows == SUB
    ctx_start = lax.axis_index("ctx") * block_rows
    local_flags = flagged - ctx_start
    experts_all = lax.axis_size("ep") * EXP_DEV
    capacity = 2 * block_rows * TOP // experts_all
    row_number = jnp.arange(block_rows, dtype=jnp.int32)
    expert_number = jnp.arange(experts_all, dtype=jnp.int32)
    named = jnp.any(expert_ids[:, :, None] == expert_number[None, None, :], axis=1)
    before = (row_number[:, None] > row_number[None, :]).astype(jnp.bfloat16)
    slot_index = jnp.dot(before, named.astype(jnp.bfloat16), preferred_element_type=jnp.float32)
    slot_index = jnp.where(named, slot_index.astype(jnp.int32), -1).T[:, None, :]
    row_flags = jnp.any(local_flags[:, None] == row_number[None, :], axis=0, keepdims=True)
    tiles = layer(
        queries,
        key_rows,
        value_rows,
        log_decay,
        out_weight,
        slot_index,
        row_flags.astype(jnp.float32),
        direction[None, :],
        capacity,
    )
    if tiles.ndim == 3:
        tiles = jnp.transpose(tiles, (1, 0, 2)).reshape(capacity, -1)
    return tiles[None]


def solution(mesh):
    placed = (
        P("ctx", "ep"),
        P("ctx", "ep"),
        P("ctx", "ep"),
        P("ctx", "ep"),
        P("ep", None),
        P("ctx", None),
        P("ctx"),
        P("ep"),
    )
    return jax.shard_map(
        local, mesh=mesh, in_specs=placed, out_specs=P("ep", "ctx", None), check_vma=False
    )
```

time: 139 us -> 62.4 us (0.45)
  waiting for transfers between devices: 61.5 us -> 0 us
  Pallas kernels: 0 us -> 54.5 us
  blocking collectives: 24 us -> 0 us
  matrix products: 18.8 us -> 0.16 us
  between operations: 14.2 us -> 0.04 us
  starting transfers between devices: 7.74 us -> 0 us
  other arithmetic: 6.58 us -> 1.45 us
    pallas_call x0 -> x1, Pallas kernels: none -> 54.5 us  [layer(): pl.pallas_call(functools.partial(layer_kernel, devices, lax.axis_size('ct...]
    all_gather x1 -> x0, waiting for transfers between devices: 41 us -> none  [local(): lax.all_gather(attended, 'ep', axis=1, tiled=True)]
    all_gather x1 -> x0, blocking collectives: 24 us -> none  [local(): whole_direction = lax.all_gather(direction, 'ep', tiled=True)]
    ppermute x3 -> x0, waiting for transfers between devices: 20.4 us -> none  [passed_along(): lax.ppermute(value, axis, [(source, source + steps) for source in range(l...]
    dot_general x5 -> x0, matrix products: 18.7 us -> none  [the longest x1 11.2 us: local(): jnp.einsum('ecr,rm->ecm', picks.astype(jnp.bfloat16), projected, preferre...]
    unnamed x12 -> x8, local copies, waits for them, and re-layouts: 0.03 us -> 5.09 us
    ppermute x3 -> x0, starting transfers between devices: 3.88 us -> none  [passed_along(): lax.ppermute(value, axis, [(source, source + steps) for source in range(l...]
    all_to_all x1 -> x0, starting transfers between devices: 3.86 us -> none  [local(): lax.all_to_all(tile_rows, 'ep', split_axis=0, concat_axis=2, tiled=True)]
  transfers between devices with their start and end apart: 5 -> 0, of which waited for: 4 -> 0; matrix products, arithmetic and copies ran while one was open for 1% -> 0% of each run, Pallas kernels for 0% -> 0%
where the time goes in v3:
time: 62.4 us; the launch traced here: 62 us
  Pallas kernels  54.5 us (87%)
  local copies, waits for them, and re-layouts  5.81 us (9%)
  other arithmetic  1.45 us (2%)
    pallas_call x1, Pallas kernels, layer(): pl.pallas_call(functools.partial(layer_kernel, devices, lax.axis_size('ct...  54.5 us
    unnamed x8, local copies, waits for them, and re-layouts  5.09 us

profile of v3, /device:TPU:25, one launch (start us, length us, event | category | flops | bytes accessed | tf_op | source)
XLA Modules:
  0.0 62.0 jit_solution(191259193297335995)
XLA Ops:
  0.0 0.7 %broadcast_subtract_fusion = s32[64]{0:T(128)S(1)} fusion(s32[64]{0:T(128)} %param.14, s32[]{:T(128)S(6)} %mul.3), kind=kLoop, calls=%fused_computation.7 | loop fusion | flops 64 | bytes 516 | tf_op jit(solution)/shard_map/sub | solution.py:424
  0.7 0.1 fusion.1
  0.8 0.7 %fusion.2 = pred[256,8]{0,1:T(8,128)(4,1)S(1)} fusion(s32[256,2]{0,1:T(2,128)} %param.13), kind=kLoop, calls=%fused_computation.6 | loop fusion | flops 6144 | bytes 4096 | tf_op jit(solution)/shard_map/reduce_or | solution.py:429
  1.5 0.7 %broadcast_in_dim.22.direction_ref = f32[1,768]{1,0:T(1,128)S(1)} reshape(f32[768]{0:T(1024)} %param.15) | data formatting | bytes 6144 | tf_op jit(solution)/shard_map/broadcast_in_dim | solution.py:442
  2.1 0.2 fusion
  2.3 0.8 %copy.11.decay_ref = f32[256,8]{1,0:T(8,128)S(1)} copy(f32[256,8]{0,1:T(8,128)} %param.11) | data formatting | bytes 16384 | tf_op args[3]
  3.2 0.0 copy-start
  3.2 1.0 %copy-done = bf16[256,1024]{1,0:T(8,128)(2,1)S(1)} copy-done((bf16[256,1024]{1,0:T(8,128)(2,1)S(1)}, bf16[256,1024]{1,0:T(8,128)(2,1)}, u32[]{:S(2)}) %copy-start) | copy-done | bytes 524312
  4.2 0.0 copy-start.1
  4.2 1.0 %copy-done.1 = bf16[256,1024]{1,0:T(8,128)(2,1)S(1)} copy-done((bf16[256,1024]{1,0:T(8,128)(2,1)S(1)}, bf16[256,1024]{1,0:T(8,128)(2,1)}, u32[]{:S(2)}) %copy-start.1) | copy-done | bytes 524312
  5.3 0.0 copy-start.2
  5.3 1.0 %copy-done.2 = bf16[256,1024]{1,0:T(8,128)(2,1)S(1)} copy-done((bf16[256,1024]{1,0:T(8,128)(2,1)S(1)}, bf16[256,1024]{1,0:T(8,128)(2,1)}, u32[]{:S(2)}) %copy-start.2) | copy-done | bytes 524312
  6.3 54.5 %shard_map.82 = bf16[128,6144]{1,0:T(8,128)(2,1)S(1)} custom-call(bf16[256,1024]{1,0:T(8,128)(2,1)S(1)} %copy-done, bf16[256,1024]{1,0:T(8,128)(2,1)S(1)} %copy-done.1, bf16[256,1024]{1,0:T(8,128)(2,1)S(1)} %copy-done.2, f32[256,8]{1,0:T(8,128)S(1)} %copy.11.decay_ref, bf16[768,8192]{1,0:T(8,128)(2,1)} %weight_hbm.1, ...), custom_call_target="tpu_custom_call" | custom-call | flops 3221225472 | bytes 12582912 | tf_op jit(solution)/shard_map/pallas_call | solution.py:381
  60.9 1.1 %copy.13 = bf16[1,128,6144]{2,1,0:T(8,128)(2,1)} copy(bf16[1,128,6144]{2,1,0:T(8,128)(2,1)S(1)} %bitcast.5) | data formatting | bytes 3145728
  (2 shorter events, 0.0 us)
Async XLA Ops:
  3.2 1.0 %copy-start = (bf16[256,1024]{1,0:T(8,128)(2,1)S(1)}, bf16[256,1024]{1,0:T(8,128)(2,1)}, u32[]{:S(2)}) copy-start(bf16[256,1024]{1,0:T(8,128)(2,1)} %query_ref.1) | copy-start | bytes 1572868
  4.2 1.0 %copy-start.1 = (bf16[256,1024]{1,0:T(8,128)(2,1)S(1)}, bf16[256,1024]{1,0:T(8,128)(2,1)}, u32[]{:S(2)}) copy-start(bf16[256,1024]{1,0:T(8,128)(2,1)} %key_ref.1) | copy-start | bytes 1572868
  5.3 1.0 %copy-start.2 = (bf16[256,1024]{1,0:T(8,128)(2,1)S(1)}, bf16[256,1024]{1,0:T(8,128)(2,1)}, u32[]{:S(2)}) copy-start(bf16[256,1024]{1,0:T(8,128)(2,1)} %value_ref.1) | copy-start | bytes 1572868

commit v4 on v3

--- a/solution.py
+++ b/solution.py
@@ -22,16 +22,20 @@
     devices,
     blocks_of_sequence,
     capacity,
-    query_ref,
-    key_ref,
-    value_ref,
+    query_hbm,
+    key_hbm,
+    value_hbm,
     decay_ref,
     weight_hbm,
-    slot_ref,
-    flag_ref,
+    named_ref,
+    flagged_ref,
     direction_ref,
     out_ref,
     weight,
+    heads_in,
+    inside,
+    growth,
+    states,
     cumulated,
     cumulated_rows,
     incoming,
@@ -45,6 +49,7 @@
     products,
     directions,
     weight_sem,
+    heads_sem,
     state_send,
     state_recv,
     block_send,
@@ -59,12 +64,24 @@
     core = lax.rem(me, 2)
     turn = 1 - 2 * core
     sibling = me + turn
-    rows, width = query_ref.shape
+    rows, width = query_hbm.shape
+    half = width // 2
     heads = width // HEAD
     cols = weight.shape[0]
     pairs = devices // 2
     has_next = place < blocks_of_sequence - 1
 
+    def heads_copy(side, which):
+        source = (query_hbm, key_hbm, value_hbm)[which]
+        return pltpu.make_async_copy(
+            source.at[:, pl.ds(side * half, half)],
+            heads_in.at[side, which],
+            heads_sem.at[side, which],
+        )
+
+    for side in range(2):
+        for which in range(3):
+            heads_copy(side, which).start()
     load = pltpu.make_async_copy(weight_hbm, weight, weight_sem)
     load.start()
     barrier = pltpu.get_barrier_semaphore()
@@ -84,14 +101,14 @@
     t_index = lax.broadcasted_iota(jnp.int32, (rows, rows), 0)
     s_index = lax.broadcasted_iota(jnp.int32, (rows, rows), 1)
     causal = t_index >= s_index
-    lower = jnp.where(causal, 1.0, 0.0)
-    cumulated[...] = jnp.dot(
-        lower,
+    upper = jnp.where(t_index <= s_index, 1.0, 0.0)
+    whole_rows = jnp.dot(
         decay_ref[...],
+        upper,
         precision=lax.Precision.HIGHEST,
         preferred_element_type=jnp.float32,
     )
-    whole_rows = jnp.transpose(cumulated[...])
+    cumulated[...] = jnp.transpose(whole_rows)
     for head in range(heads):
         cumulated_rows[head] = whole_rows[head : head + 1, :]
 
@@ -123,16 +140,16 @@
 
     head_lane = lax.broadcasted_iota(jnp.int32, (rows, heads), 1)
 
-    def attend(side, step, carry):
+    def within(side, step, carry):
         head = side * (heads // 2) + step
-        columns = pl.ds(pl.multiple_of(head * HEAD, HEAD), HEAD)
-        query, key, value = query_ref[:, columns], key_ref[:, columns], value_ref[:, columns]
+        columns = pl.ds(pl.multiple_of(step * HEAD, HEAD), HEAD)
+        query, key, value = (heads_in[side, which, :, columns] for which in range(3))
         level = jnp.sum(
             jnp.where(head_lane == head, cumulated[...], 0.0), axis=1, keepdims=True
         )
         last = level[rows - 1 :, :]
         key_scaled = (key.astype(jnp.float32) * jnp.exp(last - level)).astype(jnp.bfloat16)
-        state = lax.dot_general(
+        states[head] = lax.dot_general(
             key_scaled, value, (((0,), (0,)), ((), ())), preferred_element_type=jnp.float32
         )
         scores = lax.dot_general(
@@ -140,32 +157,44 @@
         )
         gaps = jnp.minimum(level - cumulated_rows[head], 0.0)
         weights = jnp.where(causal, scores * jnp.exp(gaps), 0.0).astype(jnp.bfloat16)
-        inside = jnp.dot(weights, value, preferred_element_type=jnp.float32)
-
-        @pl.when(place == 0)
-        def _():
-            incoming[head] = jnp.zeros((HEAD, HEAD), jnp.bfloat16)
+        inside[head] = jnp.dot(weights, value, preferred_element_type=jnp.float32)
+        growth[head] = jnp.exp(level)
+        return carry
+
+    def pass_on(side, step, carry):
+        head = side * (heads // 2) + step
 
         @pl.when(place > 0)
         def _():
             landing = incoming.at[head]
             pltpu.make_async_copy(landing, landing, state_recv.at[head]).wait()
 
-        before = incoming[head]
-
         @pl.when(has_next)
         def _():
-            outgoing[head] = (jnp.exp(last) * before.astype(jnp.float32) + state).astype(
+            gain = growth[head, rows - 1 :, :]
+            outgoing[head] = (gain * incoming[head].astype(jnp.float32) + states[head]).astype(
                 jnp.bfloat16
             )
             state_copy(head).start()
 
-        carried = jnp.dot(query, before, preferred_element_type=jnp.float32)
-        outputs = inside + jnp.exp(level) * carried
+        return carry
+
+    def across(side, step, carry):
+        head = side * (heads // 2) + step
+        columns = pl.ds(pl.multiple_of(step * HEAD, HEAD), HEAD)
+        carried = jnp.dot(
+            heads_in[side, 0, :, columns], incoming[head], preferred_element_type=jnp.float32
+        )
+        outputs = inside[head] + growth[head] * carried
         mean_square = jnp.mean(outputs * outputs, axis=1, keepdims=True)
-        own = pl.ds(pl.multiple_of(step * HEAD, HEAD), HEAD)
-        attended[side, :, own] = (outputs * lax.rsqrt(mean_square + 1e-06)).astype(jnp.bfloat16)
-        return carry
+        attended[side, :, columns] = (outputs * lax.rsqrt(mean_square + 1e-06)).astype(
+            jnp.bfloat16
+        )
+        return carry
+
+    @pl.when(place == 0)
+    def _():
+        incoming[...] = jnp.zeros(incoming.shape, incoming.dtype)
 
     sends = []
     if relayed(devices):
@@ -275,10 +304,13 @@
 
     begin, take = exchange(attended, gathered, block_send, block_recv)
     for side in range(2):
-        lax.fori_loop(0, heads // 2, functools.partial(attend, side), 0)
+        for which in range(3):
+            heads_copy(side, which).wait()
+        count = heads // 2
+        lax.fori_loop(0, count, functools.partial(within, side), 0, unroll=True)
+        lax.fori_loop(0, count, functools.partial(pass_on, side), 0)
+        lax.fori_loop(0, count, functools.partial(across, side), 0, unroll=True)
         begin(side)
-
-    half = width // 2
 
     def multiplied(block, origin):
         result = None
@@ -308,9 +340,25 @@
         begin(side)
 
     slots = lax.broadcasted_iota(jnp.int32, (capacity, rows), 0)
-    picked = slot_ref[me] == slots
+    named = jnp.max(jnp.where(named_ref[...] == me, 1.0, 0.0), axis=0, keepdims=True)
+    earlier = jnp.where(t_index < s_index, 1.0, 0.0).astype(jnp.bfloat16)
+    slot = jnp.dot(
+        jnp.broadcast_to(named, (16, rows)).astype(jnp.bfloat16),
+        earlier,
+        preferred_element_type=jnp.float32,
+    )[0:1, :]
+    slot = jnp.where(named > 0.5, slot, -1.0).astype(jnp.int32)
+    picked = slot == slots
     picks = jnp.where(picked, 1.0, 0.0).astype(jnp.bfloat16)
-    flags = jnp.sum(jnp.where(picked, flag_ref[...], 0.0), axis=1, keepdims=True) > 0.5
+    row_number = lax.broadcasted_iota(jnp.int32, (1, rows), 1) + place * rows
+
+    def flag(index, flags):
+        return jnp.where(row_number == flagged_ref[index], 1.0, flags)
+
+    row_flags = lax.fori_loop(
+        0, flagged_ref.shape[0], flag, jnp.zeros((1, rows), jnp.float32), unroll=8
+    )
+    flags = jnp.sum(jnp.where(picked, row_flags, 0.0), axis=1, keepdims=True) > 0.5
 
     def direction_wait(step, carry):
         origin = lax.rem(me + step, devices)
@@ -368,7 +416,7 @@
 
 
 def layer(
-    queries, key_rows, value_rows, log_decay, out_weight, slot_index, row_flags, direction, capacity
+    queries, key_rows, value_rows, decay, out_weight, named, flagged, direction, capacity
 ):
     devices = lax.axis_size("ep")
     rows, width = queries.shape
@@ -377,14 +425,19 @@
     copies = 16 if relayed(devices) else 2 * devices
     shape = (devices, capacity, cols) if cols % 128 else (capacity, devices * cols)
     vmem = pl.BlockSpec(memory_space=pltpu.VMEM)
+    hbm = pl.BlockSpec(memory_space=pl.ANY)
     dma = pltpu.SemaphoreType.DMA
     return pl.pallas_call(
         functools.partial(layer_kernel, devices, lax.axis_size("ctx"), capacity),
         out_shape=jax.ShapeDtypeStruct(shape, jnp.bfloat16),
-        in_specs=[vmem] * 4 + [pl.BlockSpec(memory_space=pl.ANY)] + [vmem] * 3,
+        in_specs=[hbm] * 3 + [vmem, hbm, vmem, pl.BlockSpec(memory_space=pltpu.SMEM), vmem],
         out_specs=vmem,
         scratch_shapes=[
             pltpu.VMEM(out_weight.shape, jnp.bfloat16),
+            pltpu.VMEM((2, 3, rows, width // 2), jnp.bfloat16),
+            pltpu.VMEM((heads, rows, HEAD), jnp.float32),
+            pltpu.VMEM((heads, rows, 1), jnp.float32),
+            pltpu.VMEM((heads, HEAD, HEAD), jnp.float32),
             pltpu.VMEM((rows, heads), jnp.float32),
             pltpu.VMEM((heads, 1, rows), jnp.float32),
             pltpu.VMEM((heads, HEAD, HEAD), jnp.bfloat16),
@@ -398,6 +451,7 @@
             pltpu.VMEM((capacity, 1), jnp.float32),
             pltpu.VMEM((devices, 1, cols), jnp.float32),
             dma,
+            dma((2, 3)),
             dma((heads,)),
             dma((heads,)),
             dma((copies,)),
@@ -408,37 +462,28 @@
             dma((devices,)),
         ],
         compiler_params=pltpu.CompilerParams(
-            collective_id=0, has_side_effects=True, vmem_limit_bytes=44 * 1024 * 1024
+            collective_id=0, has_side_effects=True, vmem_limit_bytes=58 * 1024 * 1024
         ),
         cost_estimate=pl.CostEstimate(
             flops=2 * rows * devices * width * cols, bytes_accessed=out_weight.size * 2,
             transcendentals=0,
         ),
-    )(queries, key_rows, value_rows, log_decay, out_weight, slot_index, row_flags, direction)
+    )(queries, key_rows, value_rows, decay, out_weight, named, flagged, direction)
 
 
 def local(queries, key_rows, value_rows, log_decay, out_weight, expert_ids, flagged, direction):
     block_rows = queries.shape[0]
     assert block_rows == SUB
-    ctx_start = lax.axis_index("ctx") * block_rows
-    local_flags = flagged - ctx_start
     experts_all = lax.axis_size("ep") * EXP_DEV
     capacity = 2 * block_rows * TOP // experts_all
-    row_number = jnp.arange(block_rows, dtype=jnp.int32)
-    expert_number = jnp.arange(experts_all, dtype=jnp.int32)
-    named = jnp.any(expert_ids[:, :, None] == expert_number[None, None, :], axis=1)
-    before = (row_number[:, None] > row_number[None, :]).astype(jnp.bfloat16)
-    slot_index = jnp.dot(before, named.astype(jnp.bfloat16), preferred_element_type=jnp.float32)
-    slot_index = jnp.where(named, slot_index.astype(jnp.int32), -1).T[:, None, :]
-    row_flags = jnp.any(local_flags[:, None] == row_number[None, :], axis=0, keepdims=True)
     tiles = layer(
         queries,
         key_rows,
         value_rows,
-        log_decay,
+        log_decay.T,
         out_weight,
-        slot_index,
-        row_flags.astype(jnp.float32),
+        expert_ids.T,
+        flagged,
         direction[None, :],
         capacity,
     )

time: 62.4 us -> 62.3 us (level)
  Pallas kernels: 54.5 us -> 58.1 us
  local copies, waits for them, and re-layouts: 5.81 us -> 3.96 us
  other arithmetic: 1.45 us -> 0 us
    pallas_call x1, Pallas kernels: 54.5 us -> 58.1 us  [layer(): pl.pallas_call(functools.partial(layer_kernel, devices, lax.axis_size('ct...]
    unnamed x8 -> x1, local copies, waits for them, and re-layouts: 5.09 us -> 2.69 us
    reduce_or x2 -> x0, other arithmetic: 0.79 us -> none  [the longest x1 0.69 us: local(): jnp.any(expert_ids[:, :, None] == expert_number[None, None, :], axis=1)]
    sub x1 -> x0, other arithmetic: 0.66 us -> none  [local(): local_flags = flagged - ctx_start]
where the time goes in v4:
time: 62.3 us; the launch traced here: 62.1 us
  Pallas kernels  58.1 us (93%)
  local copies, waits for them, and re-layouts  3.96 us (6%)
    pallas_call x1, Pallas kernels, layer(): pl.pallas_call(functools.partial(layer_kernel, devices, lax.axis_size('ct...  58.1 us
    unnamed x1, local copies, waits for them, and re-layouts  2.69 us
    broadcast_in_dim x1, local copies, waits for them, and re-layouts, local(): direction[None, :]  1.27 us

profile of v4, /device:TPU:25, one launch (start us, length us, event | category | flops | bytes accessed | tf_op | source)
XLA Modules:
  0.0 62.1 jit_solution(15737623901627732969)
XLA Ops:
  0.0 1.3 %broadcast_in_dim.6.direction_ref = f32[1,768]{1,0:T(1,128)} reshape(f32[768]{0:T(1024)} %param.15) | data formatting | bytes 6144 | tf_op jit(solution)/shard_map/broadcast_in_dim | solution.py:487
  1.3 58.1 %shard_map.82 = bf16[128,6144]{1,0:T(8,128)(2,1)} custom-call(bf16[256,1024]{1,0:T(8,128)(2,1)} %query_hbm.1, bf16[256,1024]{1,0:T(8,128)(2,1)} %key_hbm.1, bf16[256,1024]{1,0:T(8,128)(2,1)} %value_hbm.1, f32[8,256]{1,0:T(8,128)} %bitcast.4, bf16[768,8192]{1,0:T(8,128)(2,1)} %weight_hbm.1, s32[2,256]{1,0:T(2,128)} %bitcast.5, s32[64]{0:T(128)} %flagged_ref.1, ...), custom_call_target="tpu_custom_call" | custom-call | flops 3221225472 | bytes 12582912 | tf_op jit(solution)/shard_map/pallas_call | solution.py:430
  59.4 2.7 %copy.10 = bf16[1,128,6144]{2,1,0:T(8,128)(2,1)} copy(bf16[1,128,6144]{2,1,0:T(8,128)(2,1)} %bitcast.3) | data formatting | bytes 3145728

commit v5 on v4

--- a/solution.py
+++ b/solution.py
@@ -34,6 +34,7 @@
     weight,
     heads_in,
     inside,
+    levels,
     growth,
     states,
     cumulated,
@@ -140,44 +141,65 @@
 
     head_lane = lax.broadcasted_iota(jnp.int32, (rows, heads), 1)
 
+    def update(side, step, carry):
+        head = side * (heads // 2) + step
+        columns = pl.ds(pl.multiple_of(step * HEAD, HEAD), HEAD)
+        key, value = heads_in[side, 1, :, columns], heads_in[side, 2, :, columns]
+        level = jnp.sum(
+            jnp.where(head_lane == head, cumulated[...], 0.0), axis=1, keepdims=True
+        )
+        last = level[rows - 1 :, :]
+        key_scaled = (key.astype(jnp.float32) * jnp.exp(last - level)).astype(jnp.bfloat16)
+        states[head] = lax.dot_general(
+            key_scaled, value, (((0,), (0,)), ((), ())), preferred_element_type=jnp.float32
+        )
+        levels[head] = level
+        growth[head] = jnp.exp(level)
+        return carry
+
     def within(side, step, carry):
         head = side * (heads // 2) + step
         columns = pl.ds(pl.multiple_of(step * HEAD, HEAD), HEAD)
         query, key, value = (heads_in[side, which, :, columns] for which in range(3))
-        level = jnp.sum(
-            jnp.where(head_lane == head, cumulated[...], 0.0), axis=1, keepdims=True
-        )
-        last = level[rows - 1 :, :]
-        key_scaled = (key.astype(jnp.float32) * jnp.exp(last - level)).astype(jnp.bfloat16)
-        states[head] = lax.dot_general(
-            key_scaled, value, (((0,), (0,)), ((), ())), preferred_element_type=jnp.float32
-        )
         scores = lax.dot_general(
             query, key, (((1,), (1,)), ((), ())), preferred_element_type=jnp.float32
         )
-        gaps = jnp.minimum(level - cumulated_rows[head], 0.0)
+        gaps = jnp.minimum(levels[head] - cumulated_rows[head], 0.0)
         weights = jnp.where(causal, scores * jnp.exp(gaps), 0.0).astype(jnp.bfloat16)
         inside[head] = jnp.dot(weights, value, preferred_element_type=jnp.float32)
-        growth[head] = jnp.exp(level)
-        return carry
-
-    def pass_on(side, step, carry):
-        head = side * (heads // 2) + step
-
-        @pl.when(place > 0)
-        def _():
-            landing = incoming.at[head]
-            pltpu.make_async_copy(landing, landing, state_recv.at[head]).wait()
-
-        @pl.when(has_next)
-        def _():
+        return carry
+
+    def state_wait(head):
+        landing = incoming.at[head]
+        pltpu.make_async_copy(landing, landing, state_recv.at[head]).wait()
+
+    def pass_on(side):
+        def step_on(step, carry):
+            head = side * (heads // 2) + step
+
+            @pl.when(place > 0)
+            def _():
+                state_wait(head)
+
             gain = growth[head, rows - 1 :, :]
             outgoing[head] = (gain * incoming[head].astype(jnp.float32) + states[head]).astype(
                 jnp.bfloat16
             )
             state_copy(head).start()
-
-        return carry
+            return carry
+
+        @pl.when(has_next)
+        def _():
+            lax.fori_loop(0, heads // 2, step_on, 0)
+
+    def receive_last(side):
+        def step_on(step, carry):
+            state_wait(side * (heads // 2) + step)
+            return carry
+
+        @pl.when((place > 0) & jnp.logical_not(has_next))
+        def _():
+            lax.fori_loop(0, heads // 2, step_on, 0)
 
     def across(side, step, carry):
         head = side * (heads // 2) + step
@@ -303,12 +325,18 @@
         return begin, take
 
     begin, take = exchange(attended, gathered, block_send, block_recv)
+    count = heads // 2
     for side in range(2):
         for which in range(3):
             heads_copy(side, which).wait()
-        count = heads // 2
+        lax.fori_loop(0, count, functools.partial(update, side), 0, unroll=True)
+        if side == 0:
+            pass_on(side)
+    for side in range(2):
+        if side == 1:
+            pass_on(side)
         lax.fori_loop(0, count, functools.partial(within, side), 0, unroll=True)
-        lax.fori_loop(0, count, functools.partial(pass_on, side), 0)
+        receive_last(side)
         lax.fori_loop(0, count, functools.partial(across, side), 0, unroll=True)
         begin(side)
 
@@ -436,6 +464,7 @@
             pltpu.VMEM(out_weight.shape, jnp.bfloat16),
             pltpu.VMEM((2, 3, rows, width // 2), jnp.bfloat16),
             pltpu.VMEM((heads, rows, HEAD), jnp.float32),
+            pltpu.VMEM((heads, rows, 1), jnp.float32),
             pltpu.VMEM((heads, rows, 1), jnp.float32),
             pltpu.VMEM((heads, HEAD, HEAD), jnp.float32),
             pltpu.VMEM((rows, heads), jnp.float32),
@@ -462,7 +491,7 @@
             dma((devices,)),
         ],
         compiler_params=pltpu.CompilerParams(
-            collective_id=0, has_side_effects=True, vmem_limit_bytes=58 * 1024 * 1024
+            collective_id=0, has_side_effects=True, vmem_limit_bytes=44 * 1024 * 1024
         ),
         cost_estimate=pl.CostEstimate(
             flops=2 * rows * devices * width * cols, bytes_accessed=out_weight.size * 2,

time: 62.3 us -> 63.7 us (1.022)
  local copies, waits for them, and re-layouts: 3.96 us -> 6.99 us
  Pallas kernels: 58.1 us -> 56.3 us
    unnamed x1 -> x13, local copies, waits for them, and re-layouts: 2.69 us -> 6.3 us
    pallas_call x1, Pallas kernels: 58.1 us -> 56.3 us  [layer(): pl.pallas_call(functools.partial(layer_kernel, devices, lax.axis_size('ct...]
where the time goes in v5:
time: 63.7 us; the launch traced here: 63.3 us
  Pallas kernels  56.3 us (88%)
  local copies, waits for them, and re-layouts  6.99 us (11%)
    pallas_call x1, Pallas kernels, layer(): pl.pallas_call(functools.partial(layer_kernel, devices, lax.axis_size('ct...  56.3 us
    unnamed x13, local copies, waits for them, and re-layouts  6.3 us

profile of v5, /device:TPU:25, one launch (start us, length us, event | category | flops | bytes accessed | tf_op | source)
XLA Modules:
  0.0 63.3 jit_solution(15829862709059600546)
XLA Ops:
  0.0 0.7 %broadcast_in_dim.6.direction_ref = f32[1,768]{1,0:T(1,128)S(1)} reshape(f32[768]{0:T(1024)} %param.15) | data formatting | bytes 6144 | tf_op jit(solution)/shard_map/broadcast_in_dim | solution.py:516
  0.7 0.0 copy-start
  0.7 1.0 %copy-done = bf16[256,1024]{1,0:T(8,128)(2,1)S(1)} copy-done((bf16[256,1024]{1,0:T(8,128)(2,1)S(1)}, bf16[256,1024]{1,0:T(8,128)(2,1)}, u32[]{:S(2)}) %copy-start) | copy-done | bytes 524312
  1.7 0.0 copy-start.1
  1.7 1.0 %copy-done.1 = bf16[256,1024]{1,0:T(8,128)(2,1)S(1)} copy-done((bf16[256,1024]{1,0:T(8,128)(2,1)S(1)}, bf16[256,1024]{1,0:T(8,128)(2,1)}, u32[]{:S(2)}) %copy-start.1) | copy-done | bytes 524312
  2.8 0.0 copy-start.2
  2.8 1.0 %copy-done.2 = bf16[256,1024]{1,0:T(8,128)(2,1)S(1)} copy-done((bf16[256,1024]{1,0:T(8,128)(2,1)S(1)}, bf16[256,1024]{1,0:T(8,128)(2,1)}, u32[]{:S(2)}) %copy-start.2) | copy-done | bytes 524312
  3.8 0.0 copy-start.3
  3.8 0.7 %copy-done.3 = f32[256,8]{0,1:T(8,128)S(1)} copy-done((f32[256,8]{0,1:T(8,128)S(1)}, f32[256,8]{0,1:T(8,128)}, u32[]{:S(2)}) %copy-start.3) | copy-done | bytes 8216
  4.5 0.0 copy-start.4
  4.5 0.7 %copy-done.4 = s32[256,2]{0,1:T(2,128)S(1)} copy-done((s32[256,2]{0,1:T(2,128)S(1)}, s32[256,2]{0,1:T(2,128)}, u32[]{:S(2)}) %copy-start.4) | copy-done | bytes 2072
  5.2 0.0 copy-start.5
  5.2 0.7 %copy-done.5 = s32[64]{0:T(128)S(1)} copy-done((s32[64]{0:T(128)S(1)}, s32[64]{0:T(128)}, u32[]{:S(2)}) %copy-start.5) | copy-done | bytes 280
  5.9 56.3 %shard_map.82 = bf16[128,6144]{1,0:T(8,128)(2,1)S(1)} custom-call(bf16[256,1024]{1,0:T(8,128)(2,1)S(1)} %copy-done, bf16[256,1024]{1,0:T(8,128)(2,1)S(1)} %copy-done.1, bf16[256,1024]{1,0:T(8,128)(2,1)S(1)} %copy-done.2, f32[8,256]{1,0:T(8,128)S(1)} %bitcast.4, bf16[768,8192]{1,0:T(8,128)(2,1)} %weight_hbm.1, s32[2,256]{1,0:T(2,128)S(1)} %bitcast.5, ...), custom_call_target="tpu_custom_call" | custom-call | flops 3221225472 | bytes 12582912 | tf_op jit(solution)/shard_map/pallas_call | solution.py:458
  62.2 1.1 %copy.10 = bf16[1,128,6144]{2,1,0:T(8,128)(2,1)} copy(bf16[1,128,6144]{2,1,0:T(8,128)(2,1)S(1)} %bitcast.3) | data formatting | bytes 3145728
Async XLA Ops:
  0.7 1.0 %copy-start = (bf16[256,1024]{1,0:T(8,128)(2,1)S(1)}, bf16[256,1024]{1,0:T(8,128)(2,1)}, u32[]{:S(2)}) copy-start(bf16[256,1024]{1,0:T(8,128)(2,1)} %query_hbm.1) | copy-start | bytes 1572868
  1.7 1.0 %copy-start.1 = (bf16[256,1024]{1,0:T(8,128)(2,1)S(1)}, bf16[256,1024]{1,0:T(8,128)(2,1)}, u32[]{:S(2)}) copy-start(bf16[256,1024]{1,0:T(8,128)(2,1)} %key_hbm.1) | copy-start | bytes 1572868
  2.8 1.0 %copy-start.2 = (bf16[256,1024]{1,0:T(8,128)(2,1)S(1)}, bf16[256,1024]{1,0:T(8,128)(2,1)}, u32[]{:S(2)}) copy-start(bf16[256,1024]{1,0:T(8,128)(2,1)} %value_hbm.1) | copy-start | bytes 1572868
  3.8 0.7 %copy-start.3 = (f32[256,8]{0,1:T(8,128)S(1)}, f32[256,8]{0,1:T(8,128)}, u32[]{:S(2)}) copy-start(f32[256,8]{0,1:T(8,128)} %param.11) | copy-start | bytes 24580
  4.5 0.7 %copy-start.4 = (s32[256,2]{0,1:T(2,128)S(1)}, s32[256,2]{0,1:T(2,128)}, u32[]{:S(2)}) copy-start(s32[256,2]{0,1:T(2,128)} %param.13) | copy-start | bytes 6148
  5.2 0.7 %copy-start.5 = (s32[64]{0:T(128)S(1)}, s32[64]{0:T(128)}, u32[]{:S(2)}) copy-start(s32[64]{0:T(128)} %flagged_ref.1) | copy-start | bytes 772
